TPU v7x, 256 devices: a whole 4x4x8 slice. The times are simulated.
256 devices in a mesh: seq: 8 (over y_lo, x), pos: 32 (over z, y_hi, core).
Axes of the slice: x: 4, y: 4 (y_hi: 2, y_lo: 2; y = y_hi * 2 + y_lo), z: 8, core: 2. Of those that a mesh axis runs over, the one named last changes fastest.
Arguments:
- y_rows: bfloat16 [64, 512, 3072], P('seq', 'pos'), may hold values from -6 to 6
- grad_res: bfloat16 [64, 512, 3072], P('seq', 'pos'), may hold values from -6 to 6
- shift: float32 [3072], replicated, may hold values from -3 to 3
- scale_mod: float32 [3072], replicated, may hold values from -0.5 to 0.5
- temporal_qkv: bfloat16 [3, 16, 64, 512, 128], P(None, 'seq', None, 'pos'), may hold values from -6 to 6
- temporal_grad: bfloat16 [16, 64, 512, 128], P('seq', None, 'pos'), may hold values from -6 to 6
- spatial_qkv: bfloat16 [3, 16, 64, 512, 128], P(None, 'seq', 'pos'), may hold values from -6 to 6
- spatial_out: bfloat16 [16, 64, 512, 128], P('seq', None, 'pos'), may hold values from -6 to 6
- w_temporal: bfloat16 [16, 3072, 3, 128], P('seq', 'pos'), may hold values from -0.109375 to 0.109375
- w_spatial: bfloat16 [16, 3072, 128], P('seq', 'pos'), may hold values from -0.125 to 0.125
Outputs:
- spatial_grads: bfloat16 [3, 16, 64, 512, 128], P(None, 'seq', None, 'pos')
- input_grad: bfloat16 [64, 512, 3072], P('seq', 'pos')
- w_temporal_grad: float32 [16, 3072, 3, 128], P('seq', 'pos')
- w_spatial_grad: float32 [16, 3072, 128], P('seq', 'pos')
All inputs are finite; a program needn't handle non-finite values.
Results may differ from a plain program's by a relative error of at most 0.03.
Values may be sent and summed in bfloat16 or wider, within the bound.
A program may use at most 128 MiB of HBM per device.

v0:
```python
import jax
import jax.numpy as jnp
from jax import lax
from jax.sharding import PartitionSpec as P


def normalize(rows, shift, scale_mod):
    values = rows.astype(jnp.float32)
    center = values - jnp.mean(values, axis=-1, keepdims=True)
    inverse = lax.rsqrt(jnp.mean(center * center, axis=-1, keepdims=True) + 1e-06)
    unit_rows = center * inverse
    normed = (unit_rows * (1.0 + scale_mod) + shift).astype(jnp.bfloat16)
    return (normed, unit_rows, inverse)


def norm_back(grad_normed, unit_rows, inverse, scale_mod):
    scaled = grad_normed * (1.0 + scale_mod)
    first_mean = jnp.mean(scaled, axis=-1, keepdims=True)
    second_mean = jnp.mean(scaled * unit_rows, axis=-1, keepdims=True)
    return inverse * (scaled - first_mean - unit_rows * second_mean)


def attention_back(queries, key_rows, value_rows, grad_out):
    factor = queries.shape[-1] ** (-0.5)
    scores = (
        jnp.einsum("...ie,...je->...ij", queries, key_rows, preferred_element_type=jnp.float32)
        * factor
    )
    highest = jnp.max(scores, axis=-1, keepdims=True)
    exponent = jnp.exp(scores - highest)
    attend = exponent / jnp.sum(exponent, axis=-1, keepdims=True)
    attend_low = attend.astype(jnp.bfloat16)
    grad_values = jnp.einsum(
        "...ij,...ie->...je", attend_low, grad_out, preferred_element_type=jnp.float32
    )
    grad_attend = jnp.einsum(
        "...ie,...je->...ij", grad_out, value_rows, preferred_element_type=jnp.float32
    )
    inner = jnp.sum(attend * grad_attend, axis=-1, keepdims=True)
    grad_scores = (attend * (grad_attend - inner) * factor).astype(jnp.bfloat16)
    grad_queries = jnp.einsum(
        "...ij,...je->...ie", grad_scores, key_rows, preferred_element_type=jnp.float32
    )
    grad_keys = jnp.einsum(
        "...ij,...ie->...je", grad_scores, queries, preferred_element_type=jnp.float32
    )
    return jnp.stack([grad_queries, grad_keys, grad_values]).astype(jnp.bfloat16)


def local(
    y_rows,
    grad_res,
    shift,
    scale_mod,
    temporal_qkv,
    temporal_grad,
    spatial_qkv,
    spatial_out,
    w_temporal,
    w_spatial,
):
    temporal_full, spatial_full = (
        lax.all_gather(w_temporal, "pos", axis=1, tiled=True),
        lax.all_gather(w_spatial, "pos", axis=1, tiled=True),
    )
    frames_dev = y_rows.shape[0]
    rows_all = lax.all_gather(y_rows, "seq", axis=0, tiled=True)
    normed, unit_rows, inverse = normalize(rows_all, shift, scale_mod)
    swapped = jnp.swapaxes(temporal_qkv, 2, 3)
    grads_t = attention_back(swapped[0], swapped[1], swapped[2], jnp.swapaxes(temporal_grad, 1, 2))
    grads_t = jnp.swapaxes(grads_t, 2, 3)
    temporal_wgrad = jnp.einsum(
        "fpd,chfpe->hdce", normed, grads_t, preferred_element_type=jnp.float32
    )
    first_frame = lax.axis_index("seq") * frames_dev
    summed = lax.psum_scatter(
        jnp.einsum(
            "chfpe,hdce->fpd", grads_t, temporal_full, preferred_element_type=jnp.float32
        ).astype(jnp.bfloat16),
        "seq",
        scatter_dimension=0,
        tiled=True,
    ).astype(jnp.float32)
    own_unit = lax.dynamic_slice_in_dim(unit_rows, first_frame, frames_dev, 0)
    own_inverse = lax.dynamic_slice_in_dim(inverse, first_frame, frames_dev, 0)
    grad_input = grad_res.astype(jnp.float32) + norm_back(summed, own_unit, own_inverse, scale_mod)
    own_grad = grad_input.astype(jnp.bfloat16)
    grad_all = lax.all_gather(own_grad, "seq", axis=0, tiled=True)
    grad_spatial_out = jnp.einsum(
        "fpd,hde->hfpe", grad_all, spatial_full, preferred_element_type=jnp.float32
    ).astype(jnp.bfloat16)
    spatial_wgrad = jnp.einsum(
        "hfpe,fpd->hde", spatial_out, grad_all, preferred_element_type=jnp.float32
    )
    by_frames = lax.all_to_all(grad_spatial_out, "pos", split_axis=1, concat_axis=2, tiled=True)
    grads_s = attention_back(spatial_qkv[0], spatial_qkv[1], spatial_qkv[2], by_frames)
    by_heads = lax.all_to_all(grads_s, "pos", split_axis=3, concat_axis=2, tiled=True)
    temporal_sum, spatial_sum = (
        lax.psum_scatter(
            temporal_wgrad.astype(jnp.bfloat16), "pos", scatter_dimension=1, tiled=True
        ).astype(jnp.float32),
        lax.psum_scatter(
            spatial_wgrad.astype(jnp.bfloat16), "pos", scatter_dimension=1, tiled=True
        ).astype(jnp.float32),
    )
    return (by_heads, own_grad, temporal_sum, spatial_sum)


def solution(mesh):
    placed = (
        P("seq", "pos", None),
        P("seq", "pos", None),
        P(),
        P(),
        P(None, "seq", None, "pos", None),
        P("seq", None, "pos", None),
        P(None, "seq", "pos", None, None),
        P("seq", None, "pos", None),
        P("seq", "pos", None, None),
        P("seq", "pos", None),
    )
    return jax.shard_map(
        local,
        mesh=mesh,
        in_specs=placed,
        out_specs=(
            P(None, "seq", None, "pos", None),
            P("seq", "pos", None),
            P("seq", "pos", None, None),
            P("seq", "pos", None),
        ),
        check_vma=False,
    )
```

profile of v0, /device:TPU:1, one launch (start us, length us, event | category | flops | bytes accessed | tf_op | source)
XLA Modules:
  0.0 877.6 jit_solution(2780713268658229268)
XLA Ops:
  7.2 0.0 copy-start
  7.2 0.0 all-gather.7.cloned.1.call-start
  7.2 1.6 copy.31
  8.9 0.0 all-gather.7.cloned.1.call-update
  8.9 0.0 all-gather.5.cloned.1.call-start
  8.9 0.7 all-gather.5.cloned.1.call-update
  9.6 0.0 reduce-scatter.3.cloned.1.call-start
  9.7 1.8 copy.67
  11.5 1.4 fusion.124
  12.9 1.4 fusion.91
  14.4 2.9 fusion.75
  17.3 2.8 fusion.76
  20.2 1.7 fusion.77
  21.9 0.8 copy-done.7
  22.7 0.2 maximum_bitcast_fusion
  22.9 81.4 %all-gather.7.cloned.1.call-done = bf16[2,3072,3,128]{3,1,0,2:T(8,128)(2,1)} async-done(((bf16[2,96,3,128]{3,1,0,2:T(8,128)(2,1)}), bf16[2,3072,3,128]{3,1,0,2:T(8,128)(2,1)}) %all-gather.7.cloned.1.call-update) | async-done | bytes 4718608 | tf_op jit(solution)/shard_map/all_gather | solution.py:63
  104.3 11.8 %bitcast_convert_fusion = bf16[64,16,3072]{2,1,0:T(8,128)(2,1)} fusion(bf16[2,3072,3,128]{3,1,0,2:T(8,128)(2,1)} %all-gather.7.cloned.1.call-done, bf16[3,2,64,16,128]{4,2,3,1,0:T(8,128)(2,1)S(1)} %maximum_bitcast_fusion), kind=kOutput, calls=%fused_computation.9 | convolution fusion | flops 4834983936 | bytes 12582912 | tf_op jit(solution)/shard_map/chfpe,hdce->fpd/dot_general | solution.py:77
  116.1 0.0 reduce-scatter.3.cloned.1.call-update
  116.2 0.0 all-gather.11.cloned.1.call-start
  116.2 0.5 all-gather.11.cloned.1.call-update
  116.7 0.6 all-gather.9.cloned.1.call-start
  117.3 59.9 %all-gather.5.cloned.1.call-done = bf16[64,16,3072]{2,1,0:T(8,128)(2,1)} async-done(((bf16[8,16,3072]{2,1,0:T(8,128)(2,1)}), bf16[64,16,3072]{2,1,0:T(8,128)(2,1)}) %all-gather.5.cloned.1.call-update) | async-done | bytes 6291472 | tf_op jit(solution)/shard_map/all_gather | solution.py:67
  177.2 3.8 convert_reduce_fusion
  181.1 0.7 copy-done.1
  181.8 1.7 fusion.6
  183.7 0.0 copy-start.4
  183.7 13.4 %fusion.7 = (bf16[64,16,3072,1,1]{2,1,0,4,3:T(8,128)(2,1)}, f32[64,16,3072]{2,1,0:T(8,128)}) fusion(f32[3072]{0:T(1024)S(1)} %copy-done.10, f32[3072]{0:T(1024)S(1)} %broadcast_add_fusion, f32[64,16]{1,0:T(8,128)S(1)} %add_rsqrt_fusion, f32[64,16]{1,0:T(8,128)S(1)} %broadcast_multiply_fusion, bf16[64,16,3072]{2,1,0:T(8,128)(2,1)} %all-gather.5.cloned.1.call-done), kind=kLoop, calls=%fused_computation.12 | loop fusion | flops 18874368 | bytes 25198592 | tf_op jit(solution)/shard_map/convert_element_type | solution.py:12
  197.1 57.1 %reduce-scatter.3.cloned.1.call-done = bf16[8,16,3072]{2,1,0:T(8,128)(2,1)} async-done(((bf16[64,16,3072]{2,1,0:T(8,128)(2,1)}), bf16[8,16,3072]{2,1,0:T(8,128)(2,1)}) %reduce-scatter.3.cloned.1.call-update) | async-done | bytes 786448 | tf_op jit(solution)/shard_map/reduce_scatter | solution.py:76
  254.1 2.0 fusion.48
  256.1 0.0 copy-done.4
  256.1 3.1 add_convert_fusion.1
  259.2 0.0 all-gather.9.cloned.1.call-update
  259.3 75.4 %all-gather.11.cloned.1.call-done = bf16[2,3072,128]{2,1,0:T(8,128)(2,1)} async-done(((bf16[2,96,128]{2,1,0:T(8,128)(2,1)}), bf16[2,3072,128]{2,1,0:T(8,128)(2,1)}) %all-gather.11.cloned.1.call-update) | async-done | bytes 1572880 | tf_op jit(solution)/shard_map/all_gather | solution.py:64
  334.7 72.9 %all-gather.9.cloned.1.call-done = bf16[64,16,3072]{2,1,0:T(8,128)(2,1)} async-done(((bf16[8,16,3072]{2,1,0:T(8,128)(2,1)}), bf16[64,16,3072]{2,1,0:T(8,128)(2,1)}) %all-gather.9.cloned.1.call-update) | async-done | bytes 6291472 | tf_op jit(solution)/shard_map/all_gather | solution.py:88
  407.6 5.8 fusion.81
  413.4 10.0 %all-to-all-start = ((bf16[2,64,16,128]{3,2,0,1:T(8,128)(2,1)}), bf16[2,64,16,128]{3,2,0,1:T(8,128)(2,1)S(1)}, u32[]{:S(2)}, u32[]{:S(2)}) async-start(bf16[2,64,16,128]{3,2,0,1:T(8,128)(2,1)} %fusion.81), calls=%async_computation.1 | async-start | bytes 1048576 | tf_op jit(solution)/shard_map/all_to_all | solution.py:95
  423.4 0.2 all-reduce.3.cloned.1.call-start
  423.7 20.8 %fusion.17 = bf16[2,3072,3,128]{1,3,0,2:T(8,128)(2,1)} fusion(bf16[64,16,3072,1,1]{2,1,0,4,3:T(8,128)(2,1)} %get-tuple-element.14, bf16[1,2,16,64,128]{4,3,2,1,0:T(8,128)(2,1)S(1)} %copy-done.8, bf16[1,2,16,64,128]{4,3,2,1,0:T(8,128)(2,1)S(1)} %copy-done.6, bf16[1,2,16,64,128]{4,3,2,1,0:T(8,128)(2,1)S(1)} %copy-done.5), kind=kOutput, calls=%fused_computation.20 | convolution fusion | flops 4835770368 | bytes 12582912 | tf_op jit(solution)/shard_map/fpd,chfpe->hdce/dot_general | solution.py:72
  444.4 12.7 %copy.38 = bf16[2,3072,3,128]{3,0,2,1:T(2,128)(2,1)} copy(bf16[2,3072,3,128]{1,3,0,2:T(8,128)(2,1)} %fusion.17) | data formatting | bytes 9437184 | tf_op jit(solution)/shard_map/convert_element_type | solution.py:100
  457.1 0.0 copy-start.3
  457.2 0.0 all-reduce.3.cloned.1.call-update
  457.2 1.4 copy-done.3
  458.6 0.7 fusion.95
  459.3 2.1 copy-done.2
  461.4 3.1 fusion.125
  464.5 0.0 all-to-all-done
  464.5 2.7 fusion.92
  467.3 8.0 fusion.72
  475.3 5.9 fusion.78
  481.1 8.5 fusion.69
  489.7 1.2 pad_maximum_fusion
  490.9 2.8 copy.35
  493.7 9.8 %all-to-all-start.1 = ((bf16[3,2,2,512,128]{4,2,1,0,3:T(2,128)(2,1)}), bf16[3,2,2,512,128]{4,2,1,0,3:T(2,128)(2,1)S(1)}, u32[]{:S(2)}, u32[]{:S(2)}) async-start(bf16[3,2,2,512,128]{4,2,1,0,3:T(2,128)(2,1)} %copy.35), calls=%async_computation.2 | async-start | bytes 3145728 | tf_op jit(solution)/shard_map/all_to_all | solution.py:97
  503.5 0.0 copy-start.12
  503.5 0.3 reduce-scatter.5.cloned.1.call-start
  503.8 5.9 fusion.27
  509.7 0.0 reduce-scatter.5.cloned.1.call-update
  509.7 0.6 dynamic-slice.4
  511.0 241.2 %all-reduce.3.cloned.1.call-done = bf16[2,3072,3,128]{3,0,2,1:T(2,128)(2,1)} async-done(((bf16[2,3072,3,128]{3,0,2,1:T(2,128)(2,1)}), bf16[2,3072,3,128]{3,0,2,1:T(2,128)(2,1)}) %all-reduce.3.cloned.1.call-update) | async-done | bytes 4718608
  752.2 1.0 dynamic-slice_convert_fusion
  753.2 0.7 copy.41
  753.9 113.6 %reduce-scatter.5.cloned.1.call-done = bf16[2,96,128]{2,1,0:T(8,128)(2,1)} async-done(((bf16[2,3072,128]{2,1,0:T(8,128)(2,1)}), bf16[2,96,128]{2,1,0:T(8,128)(2,1)}) %reduce-scatter.5.cloned.1.call-update) | async-done | bytes 49168 | tf_op jit(solution)/shard_map/reduce_scatter | solution.py:102
  867.5 1.4 convert_element_type.73
  869.0 1.4 copy.36
  (24 shorter events, 0.1 us)
Async XLA Ops:
  7.2 496.7 %copy-start = (bf16[2,64,16,128]{3,2,1,0:T(8,128)(2,1)S(1)}, bf16[2,64,16,128]{3,2,1,0:T(8,128)(2,1)}, u32[]{:S(2)}) copy-start(bf16[2,64,16,128]{3,2,1,0:T(8,128)(2,1)} %param.17) | copy-start | bytes 1572868
  7.2 97.1 %all-gather.7.cloned.1.call-start = ((), (), s32[]{:S(2)}) async-start(), calls=%async_computation.5 | async-start | bytes 4866048 | tf_op jit(solution)/shard_map/all_gather | solution.py:63
  8.9 168.4 %all-gather.5.cloned.1.call-start = ((), (), s32[]{:S(2)}) async-start(), calls=%async_computation.4 | async-start | bytes 7077888 | tf_op jit(solution)/shard_map/all_gather | solution.py:67
  9.6 244.5 %reduce-scatter.3.cloned.1.call-start = ((), (), s32[]{:S(2)}) async-start(), calls=%async_computation.6 | async-start | bytes 7077888 | tf_op jit(solution)/shard_map/reduce_scatter | solution.py:76
  20.1 2.6 copy-start.5
  20.1 2.6 copy-start.6
  21.9 0.8 copy-start.7
  116.1 1.2 copy-start.11
  116.2 218.5 %all-gather.11.cloned.1.call-start = ((), (), s32[]{:S(2)}) async-start(), calls=%async_computation.8 | async-start | bytes 1622016 | tf_op jit(solution)/shard_map/all_gather | solution.py:64
  116.7 290.9 %all-gather.9.cloned.1.call-start = ((), (), s32[]{:S(2)}) async-start(), calls=%async_computation.7 | async-start | bytes 7077888 | tf_op jit(solution)/shard_map/all_gather | solution.py:88
  177.2 4.6 copy-start.1
  181.1 2.6 copy-start.10
  183.7 72.5 %copy-start.4 = (bf16[8,16,3072]{2,1,0:T(8,128)(2,1)S(1)}, bf16[8,16,3072]{2,1,0:T(8,128)(2,1)}, u32[]{:S(2)}) copy-start(bf16[8,16,3072]{2,1,0:T(8,128)(2,1)} %param.11) | copy-start | bytes 2359300
  259.2 164.4 %copy-start.8 = (bf16[1,2,16,64,128]{4,3,2,1,0:T(8,128)(2,1)S(1)}, bf16[1,2,16,64,128]{4,3,2,1,0:T(8,128)(2,1)}, u32[]{:S(2)}) copy-start(bf16[1,2,16,64,128]{4,3,2,1,0:T(8,128)(2,1)} %copy-done.7) | copy-start | bytes 1572868
  413.4 51.1 %all-to-all-start = ((bf16[2,64,16,128]{3,2,0,1:T(8,128)(2,1)}), bf16[2,64,16,128]{3,2,0,1:T(8,128)(2,1)S(1)}, u32[]{:S(2)}, u32[]{:S(2)}) async-start(bf16[2,64,16,128]{3,2,0,1:T(8,128)(2,1)} %fusion.81), calls=%async_computation.1 | async-start | bytes 1048576 | tf_op jit(solution)/shard_map/all_to_all | solution.py:95
  423.4 328.7 %all-reduce.3.cloned.1.call-start = ((), (), s32[]{:S(2)}) async-start(), calls=%async_computation.10 | async-start | bytes 9437184
  457.1 1.4 copy-start.3
  459.3 2.1 copy-start.2
  481.1 8.5 copy-start.9
  493.7 375.3 %all-to-all-start.1 = ((bf16[3,2,2,512,128]{4,2,1,0,3:T(2,128)(2,1)}), bf16[3,2,2,512,128]{4,2,1,0,3:T(2,128)(2,1)S(1)}, u32[]{:S(2)}, u32[]{:S(2)}) async-start(bf16[3,2,2,512,128]{4,2,1,0,3:T(2,128)(2,1)} %copy.35), calls=%async_computation.2 | async-start | bytes 3145728 | tf_op jit(solution)/shard_map/all_to_all | solution.py:97
  503.5 6.2 copy-start.12
  503.5 364.0 %reduce-scatter.5.cloned.1.call-start = ((), (), s32[]{:S(2)}) async-start(), calls=%async_computation.9 | async-start | bytes 1622016 | tf_op jit(solution)/shard_map/reduce_scatter | solution.py:102
Sparse Core Ops, SparseCore 0:
  11.3 92.9 all-gather.6
  106.1 71.1 all-gather.4
  179.8 74.2 reduce-scatter.2
  256.7 77.9 all-gather.10
  336.9 70.6 all-gather.8
  457.3 294.8 all-reduce.2
  756.2 111.2 reduce-scatter.4
where the time goes:
time: 888 us; the launch traced here: 878 us
  waiting for transfers between devices  703 us (79%)
  matrix products  80.5 us (9%)
  other arithmetic  31.1 us (4%)
  local copies, waits for them, and re-layouts  26.8 us (3%)
  starting transfers between devices  21.1 us (2%)
  between operations  15.3 us (2%)
    unnamed x8, waiting for transfers between devices  243 us
    reduce_scatter x1, waiting for transfers between devices, local(): lax.psum_scatter(spatial_wgrad.astype(jnp.bfloat16), 'pos', scatter_dimen...  114 us
    all_gather x1, waiting for transfers between devices, local(): lax.all_gather(w_temporal, 'pos', axis=1, tiled=True)  81.4 us
    all_gather x1, waiting for transfers between devices, local(): lax.all_gather(w_spatial, 'pos', axis=1, tiled=True)  75.4 us
    all_gather x1, waiting for transfers between devices, local(): grad_all = lax.all_gather(own_grad, 'seq', axis=0, tiled=True)  72.9 us
    all_gather x1, waiting for transfers between devices, local(): rows_all = lax.all_gather(y_rows, 'seq', axis=0, tiled=True)  59.9 us
    reduce_scatter x1, waiting for transfers between devices, local(): lax.psum_scatter(jnp.einsum('chfpe,hdce->fpd', grads_t, temporal_full, pr...  57.1 us
    dot_general x1, matrix products, local(): jnp.einsum('fpd,chfpe->hdce', normed, grads_t, preferred_element_type=jnp...  20.8 us
  transfers between devices with their start and end apart: 9, of which 7 were waited for; matrix products, arithmetic and copies ran while one was open for 14% of the time, Pallas kernels for 0%

commit v1 on v0

v1 whole, which is shorter than its diff:
```python
import functools

import jax
import jax.numpy as jnp
from jax import lax
from jax.experimental import pallas as pl
from jax.experimental.pallas import tpu as pltpu
from jax.sharding import PartitionSpec as P

MESH = pl.DeviceIdType.MESH
F32 = jnp.float32
BF16 = jnp.bfloat16
NT = (((1,), (1,)), ((), ()))
TN = (((0,), (0,)), ((), ()))
NN = (((1,), (0,)), ((), ()))


def dot(a, b, dims=NN):
    return lax.dot_general(a, b, dims, preferred_element_type=F32)


class Place:
    def __init__(self):
        s, p = lax.axis_index("seq"), lax.axis_index("pos")
        self.yl, self.x = s // 4, s % 4
        self.z, self.yh, self.co = p // 4, (p // 2) % 2, p % 2

    def at(self, yl=None, x=None, z=None, yh=None, co=None):
        yl = self.yl if yl is None else yl
        x = self.x if x is None else x
        z = self.z if z is None else z
        yh = self.yh if yh is None else yh
        co = self.co if co is None else co
        return (yl * 4 + x, z * 4 + yh * 2 + co)

    def dx(self, k):
        return (self.x + k + 4) % 4

    def dz(self, k):
        return (self.z + k + 8) % 8

    def neighbours(self, seq, pos):
        found = []
        if seq:
            found += [self.at(x=self.dx(1)), self.at(x=self.dx(-1)), self.at(yl=1 - self.yl)]
        if pos:
            found += [
                self.at(z=self.dz(1)),
                self.at(z=self.dz(-1)),
                self.at(yh=1 - self.yh),
                self.at(co=1 - self.co),
            ]
        return found


def meet(devices):
    barrier = pltpu.get_barrier_semaphore()
    for device in devices:
        pl.semaphore_signal(barrier, inc=1, device_id=device, device_id_type=MESH)
    pl.semaphore_wait(barrier, len(devices))


class Net:
    def __init__(self, send_sem, recv_sem):
        self.send_sem, self.recv_sem, self.count, self.open = send_sem, recv_sem, 0, []

    def send(self, source, target, device):
        i = self.count
        self.count += 1
        copy = pltpu.make_async_remote_copy(
            src_ref=source,
            dst_ref=target,
            send_sem=self.send_sem.at[i],
            recv_sem=self.recv_sem.at[i],
            device_id=device,
            device_id_type=MESH,
        )
        copy.start()
        self.open.append(copy)
        return copy

    def finish(self):
        for copy in self.open:
            copy.wait_send()
        self.open = []


def run_all(steps):
    live = list(steps)
    while live:
        for step in list(live):
            try:
                next(step)
            except StopIteration:
                live.remove(step)


def add_into(target, terms, rows, tile=16):
    def body(i, carry):
        at = pl.ds(pl.multiple_of(i * tile, tile), tile)
        total = target[at, :].astype(F32)
        for term in terms:
            total += term[at, :].astype(F32)
        target[at, :] = total.astype(BF16)
        return carry

    lax.fori_loop(0, rows // tile, body, 0)


def gather_pos(net, me, own, full):
    def slot(z, r, co):
        return full.at[z * 4 + ((me.yh + r) % 2) * 2 + co]

    up, down = me.at(z=me.dz(1)), me.at(z=me.dz(-1))
    other = me.at(co=1 - me.co)
    mine = slot(me.z, 0, me.co)
    cross = net.send(own, mine, me.at(yh=1 - me.yh))
    plus = [net.send(own, mine, up)]
    minus = [net.send(own, mine, down)]
    cores = [net.send(own, mine, other)]
    mine[...] = own[...]
    yield
    cross.wait_recv()
    near = slot(me.z, 1, me.co)
    plus.append(net.send(near, near, up))
    minus.append(net.send(near, near, down))
    cores.append(net.send(near, near, other))
    yield
    for k in range(1, 5):
        next_plus, next_minus = [], []
        for r in range(2):
            if k < 4 or r == 0:
                plus[r].wait_recv()
                block = slot(me.dz(-k), r, me.co)
                if k < 3 or (k == 3 and r == 0):
                    next_plus.append(net.send(block, block, up))
                else:
                    next_plus.append(None)
                cores.append(net.send(block, block, other))
            if k < 4 or r == 1:
                minus[r].wait_recv()
                block = slot(me.dz(k), r, me.co)
                if k < 3 or (k == 3 and r == 1):
                    next_minus.append(net.send(block, block, down))
                else:
                    next_minus.append(None)
                cores.append(net.send(block, block, other))
        plus, minus = next_plus, next_minus
        yield
    for copy in cores:
        copy.wait_recv()


def gather_seq(net, me, full, done):
    def part(yl, x, first, rows):
        return full.at[yl * 4 + x, pl.ds(first, rows), :]

    yl, x, far = me.yl, me.x, 1 - me.yl
    left, right, xo = me.dx(-1), me.dx(1), me.dx(2)
    to_r, to_l, to_y = me.at(x=right), me.at(x=left), me.at(yl=far)

    def push(block, device):
        return net.send(block, block, device)

    h0, h1 = part(yl, x, 0, 64), part(yl, x, 64, 64)
    y0 = push(h0, to_y)
    r0, l0 = push(h0, to_r), push(h0, to_l)
    y1 = push(h1, to_y)
    r1, l1 = push(h1, to_r), push(h1, to_l)
    done((yl, x))
    yield
    y0.wait_recv()
    f0 = part(far, x, 0, 64)
    rf, lf = push(f0, to_r), push(f0, to_l)
    r0.wait_recv()
    l0.wait_recv()
    ra = push(part(yl, left, 0, 32), to_r)
    lb = push(part(yl, right, 32, 32), to_l)
    y1.wait_recv()
    done((far, x))
    yield
    r1.wait_recv()
    l1.wait_recv()
    rc = push(part(yl, left, 64, 32), to_r)
    ld = push(part(yl, right, 96, 32), to_l)
    yr = push(part(yl, left, 64, 64), to_y)
    yq = push(part(yl, right, 64, 64), to_y)
    done((yl, left))
    done((yl, right))
    yield
    rf.wait_recv()
    lf.wait_recv()
    re = push(part(far, left, 0, 32), to_r)
    lg = push(part(far, right, 32, 32), to_l)
    ra.wait_recv()
    lb.wait_recv()
    yield
    rc.wait_recv()
    ld.wait_recv()
    yo = push(part(yl, xo, 64, 64), to_y)
    done((yl, xo))
    yield
    yr.wait_recv()
    yq.wait_recv()
    done((far, left))
    done((far, right))
    yield
    re.wait_recv()
    lg.wait_recv()
    yo.wait_recv()
    done((far, xo))


def reduce_x(net, me, block, quarter, half, started, result):
    left, right, xo = me.dx(-1), me.dx(1), me.dx(2)
    to_r, to_l = me.at(x=right), me.at(x=left)
    a = net.send(block(xo).at[pl.ds(0, 32)], quarter.at[0], to_r)
    b = net.send(block(xo).at[pl.ds(32, 32)], quarter.at[1], to_l)
    started()
    yield
    a.wait_recv()
    add_into(block(right).at[pl.ds(0, 32)], [quarter.at[0]], 32)
    c = net.send(block(right), half.at[0], to_r)
    b.wait_recv()
    add_into(block(left).at[pl.ds(32, 32)], [quarter.at[1]], 32)
    d = net.send(block(left), half.at[1], to_l)
    yield
    c.wait_recv()
    d.wait_recv()
    result()


def reduce_pos_ring(net, me, part, core_recv, core_copies, ring, across, out):
    up, down = me.at(z=me.dz(1)), me.at(z=me.dz(-1))

    def slot(z, r):
        return part.at[z, ((me.yh + r) % 2) * 2 + me.co]

    def merge(z, k):
        core_copies[k].wait_recv()
        for r in range(2):
            add_into(slot(z, r), [core_recv.at[z, (me.yh + r) % 2]], 96)

    merge(me.dz(4), 0)
    plus = [net.send(slot(me.dz(4), 0), ring.at[0, 0, 0], up), None]
    minus = [None, net.send(slot(me.dz(4), 1), ring.at[1, 0, 1], down)]
    merge(me.dz(3), 1)
    merge(me.dz(-3), 2)
    yield
    for k in range(1, 4):
        next_plus, next_minus = [], []
        for r in range(2):
            at = slot(me.dz(4 - k), r)
            if plus[r] is not None:
                plus[r].wait_recv()
                add_into(at, [ring.at[0, k - 1, r]], 96)
            next_plus.append(net.send(at, ring.at[0, k, r], up))
            at = slot(me.dz(k - 4), r)
            if minus[r] is not None:
                minus[r].wait_recv()
                add_into(at, [ring.at[1, k - 1, r]], 96)
            next_minus.append(net.send(at, ring.at[1, k, r], down))
        plus, minus = next_plus, next_minus
        if k < 3:
            merge(me.dz(3 - k), 2 * k + 1)
            merge(me.dz(k - 3), 2 * k + 2)
        else:
            merge(me.z, 7)
        yield
    for r in (1, 0):
        plus[r].wait_recv()
        minus[r].wait_recv()
        add_into(slot(me.z, r), [ring.at[0, 3, r], ring.at[1, 3, r]], 96)
        if r == 1:
            swap = net.send(slot(me.z, 1), across, me.at(yh=1 - me.yh))
    yield
    swap.wait_recv()
    out[...] = slot(me.z, 0)[...].astype(F32) + across[...].astype(F32)


def z_order(i):
    return 4 + (1 - 2 * (i % 2)) * ((i + 1) // 2)


def core_copy(me, part, core_recv, send_sem, recv_sem, zt, i):
    copies = []
    for yh in range(2):
        copies.append(
            pltpu.make_async_remote_copy(
                src_ref=part.at[zt, yh * 2 + 1 - me.co],
                dst_ref=core_recv.at[zt, yh],
                send_sem=send_sem.at[i, yh],
                recv_sem=recv_sem.at[i, yh],
                device_id=me.at(co=1 - me.co),
                device_id_type=MESH,
            )
        )
    return copies


class Pair:
    def __init__(self, copies):
        self.copies = copies

    def wait_recv(self):
        for copy in self.copies:
            copy.wait_recv()


def core_copies_of(me, part, core_recv, send_sem, recv_sem):
    return [
        Pair(core_copy(me, part, core_recv, send_sem, recv_sem, me.dz(z_order(i) - 8), i))
        for i in range(8)
    ]


def weight_partial(me, rows_ref, right, part, core_recv, send_sem, recv_sem):
    def body(i, carry):
        zt = (me.z + z_order(i)) % 8
        at = pl.ds(pl.multiple_of(zt * 384, 128), 384)
        left = rows_ref[:, :, at].reshape(1024, 384)
        result = dot(left, right(), TN).astype(BF16)
        part[zt] = result.reshape(4, 96, result.shape[-1])
        for copy in core_copy(me, part, core_recv, send_sem, recv_sem, zt, i):
            copy.start()
        return carry

    lax.fori_loop(0, 8, body, 0)


def attention_rows(q, k, v, g, mask):
    factor = 128**-0.5
    s = dot(q, k, NT) * factor
    if mask is not None:
        s = jnp.where(mask, s, -1e30)
    e = jnp.exp(s - jnp.max(s, axis=-1, keepdims=True))
    p = e * (1.0 / jnp.sum(e, axis=-1, keepdims=True))
    dp = dot(g, v, NT)
    inner = jnp.sum(p * dp, axis=-1, keepdims=True)
    ds = (p * (dp - inner) * factor).astype(BF16)
    return dot(ds, k), dot(ds, q, TN), dot(p.astype(BF16), g, TN)


def temporal(h, qkv, grad, dk, dv, out):
    tile = 128
    rows = lax.broadcasted_iota(jnp.int32, (tile, 1024), 0)
    cols = lax.broadcasted_iota(jnp.int32, (tile, 1024), 1)
    mask = (rows % 16) == (cols % 16)

    def body(t, carry):
        at = pl.ds(pl.multiple_of(t * tile, tile), tile)
        one, two, three = attention_rows(
            qkv[0, h, at, :], qkv[1, h], qkv[2, h], grad[h, at, :], mask
        )
        out[at, pl.ds(h * 384, 128)] = one.astype(BF16)
        dk[...] += two
        dv[...] += three
        return carry

    dk[...] = jnp.zeros_like(dk)
    dv[...] = jnp.zeros_like(dv)
    lax.fori_loop(0, 1024 // tile, body, 0)
    out[:, pl.ds(h * 384 + 128, 128)] = dk[...].astype(BF16)
    out[:, pl.ds(h * 384 + 256, 128)] = dv[...].astype(BF16)


def unit_of(y):
    values = y.astype(F32)
    center = values - jnp.mean(values, axis=-1, keepdims=True)
    inverse = lax.rsqrt(jnp.mean(center * center, axis=-1, keepdims=True) + 1e-06)
    return center * inverse, inverse


def main_kernel(
    w_ref, y_ref, res_ref, shift_ref, scale_ref, qkv_ref, grad_ref, sout_ref,
    gso_ref, ig_ref, wt_ref, ws_ref,
    wf, nf, dq, dk, dv, part, from_y, quarter, half, last_y,
    wpart, core_recv, ring, across, igf,
    send_sem, recv_sem, core_send, core_recv_sem,
):
    me = Place()
    net = Net(send_sem, recv_sem)
    s_own = me.yl * 4 + me.x
    far = 1 - me.yl
    meet(me.neighbours(True, True))

    first = gather_pos(net, me, w_ref, wf)
    next(first)

    def norm_tile(i, carry):
        at = pl.ds(pl.multiple_of(i * 16, 16), 16)
        unit, _ = unit_of(y_ref[at, :])
        nf[s_own, at, :] = (unit * (1.0 + scale_ref[...]) + shift_ref[...]).astype(BF16)
        return carry

    lax.fori_loop(0, 8, norm_tile, 0)
    second = gather_seq(net, me, nf, lambda at: None)
    next(second)
    next(first)

    temporal(0, qkv_ref, grad_ref, dk, dv, dq)
    next(second)
    next(first)
    temporal(1, qkv_ref, grad_ref, dk, dv, dq)
    run_all([first, second])

    def partial(x):
        lhs = jnp.concatenate(
            [dq[pl.ds(pl.multiple_of((yl * 4 + x) * 128, 128), 128), :] for yl in range(2)], axis=0
        )

        def body(z, carry):
            w = wf[pl.ds(z * 4, 4), :, pl.ds(0, 768)].reshape(384, 768)
            result = dot(lhs, w, NT).astype(BF16)
            at = pl.ds(pl.multiple_of(z * 384, 128), 384)
            part[x, :, at] = result[:128]
            part[4 + x, :, at] = result[128:]
            return carry

        lax.fori_loop(0, 8, body, 0)

    def h0(yl):
        return lambda x: part.at[yl * 4 + x, pl.ds(0, 64), :]

    def h1(x):
        return part.at[me.yl * 4 + x, pl.ds(64, 64), :]

    def to_partner(x):
        return net.send(
            part.at[far * 4 + x, pl.ds(64, 64), :], from_y.at[x], me.at(yl=far)
        )

    nothing = lambda: None
    swaps = {}
    order = [me.dx(2), me.dx(1), me.dx(-1), me.x]
    partial(order[0])
    keep = {}

    def ready(name):
        def mark():
            keep[name] = True

        return mark

    red_far = reduce_x(net, me, h0(far), quarter.at[0], half.at[0], nothing, ready("far"))
    next(red_far)
    swaps[0] = to_partner(order[0])
    red_own = reduce_x(net, me, h0(me.yl), quarter.at[1], half.at[1], nothing, ready("own"))
    next(red_own)
    for i in range(1, 4):
        partial(order[i])
        swaps[i] = to_partner(order[i])
    next(red_far)
    next(red_own)

    weight_partial(me, nf, lambda: dq[...], wpart, core_recv, core_send, core_recv_sem)
    core = core_copies_of(me, wpart, core_recv, core_send, core_recv_sem)
    wt_steps = reduce_pos_ring(net, me, wpart, core_recv, core, ring, across, wt_ref)

    for i in range(4):
        swaps[i].wait_recv()
        add_into(h1(order[i]), [from_y.at[order[i]]], 64)
        if i == 0:
            red_two = reduce_x(net, me, h1, quarter.at[2], half.at[2], nothing, ready("two"))
            next(red_two)
            next(wt_steps)
    next(red_two)
    for _ in red_far:
        pass
    mine = part.at[far * 4 + me.x, pl.ds(0, 64), :]
    add_into(mine, [half.at[0, 0], half.at[0, 1]], 64)
    swap = net.send(mine, last_y, me.at(yl=far))
    next(wt_steps)
    for _ in red_own:
        pass
    for _ in red_two:
        pass
    swap.wait_recv()

    def back_tile(i, carry, lower):
        base = 0 if lower else 64
        at = pl.ds(pl.multiple_of(i * 16 + base, 16), 16)
        sub = pl.ds(pl.multiple_of(i * 16, 16), 16)
        total = part[s_own, at, :].astype(F32)
        if lower:
            terms = [half.at[1, 0], half.at[1, 1], last_y]
        else:
            terms = [half.at[2, 0], half.at[2, 1]]
        for term in terms:
            total += term[sub, :].astype(F32)
        unit, inverse = unit_of(y_ref[at, :])
        scaled = total * (1.0 + scale_ref[...])
        one = jnp.mean(scaled, axis=-1, keepdims=True)
        two = jnp.mean(scaled * unit, axis=-1, keepdims=True)
        result = res_ref[at, :].astype(F32) + inverse * (scaled - one - unit * two)
        result = result.astype(BF16)
        igf[s_own, at, :] = result
        ig_ref[at, :] = result
        return carry

    lax.fori_loop(0, 4, functools.partial(back_tile, lower=True), 0)
    lax.fori_loop(0, 4, functools.partial(back_tile, lower=False), 0)

    pending = []

    def project(blocks):
        def body(i, carry):
            s = blocks[0]
            for n in range(1, len(blocks)):
                s = jnp.where(i == n, blocks[n], s)
            w = wf[:, :, pl.ds(768, 256)].reshape(3072, 256)
            gso_ref[s] = dot(igf[s], w).astype(BF16)
            return carry

        lax.fori_loop(0, len(blocks), body, 0)

    last = gather_seq(net, me, igf, lambda at: pending.append(at[0] * 4 + at[1]))
    live = [last, wt_steps]
    while live:
        for step in list(live):
            try:
                next(step)
            except StopIteration:
                live.remove(step)
            if len(pending) >= 3 or (step is last and last not in live):
                project(pending)
                pending.clear()

    def ws_tile(z, carry):
        at = pl.ds(pl.multiple_of(z * 384, 128), 384)
        left = igf[:, :, at].reshape(1024, 384)
        for h in range(2):
            ws_ref[z, :, :, pl.ds(h * 128, 128)] = (
                dot(left, sout_ref[h], TN).astype(BF16).reshape(4, 96, 128)
            )
        return carry

    lax.fori_loop(0, 8, ws_tile, 0)
    for pair in core:
        for copy in pair.copies:
            copy.wait_send()
    net.finish()


def ws_kernel(
    part_in, out_ref, part, core_recv, ring, across, send_sem, recv_sem, core_send, core_recv_sem
):
    me = Place()
    net = Net(send_sem, recv_sem)
    meet(me.neighbours(False, True))

    def body(i, carry):
        zt = (me.z + z_order(i)) % 8
        part[zt] = part_in[zt]
        for copy in core_copy(me, part, core_recv, core_send, core_recv_sem, zt, i):
            copy.start()
        return carry

    lax.fori_loop(0, 8, body, 0)
    core = core_copies_of(me, part, core_recv, core_send, core_recv_sem)
    for _ in reduce_pos_ring(net, me, part, core_recv, core, ring, across, out_ref):
        pass
    for pair in core:
        for copy in pair.copies:
            copy.wait_send()
    net.finish()


def spatial_kernel(qkv_ref, grad_ref, out_ref):
    one, two, three = attention_rows(
        qkv_ref[0, 0, 0], qkv_ref[1, 0, 0], qkv_ref[2, 0, 0], grad_ref[0], None
    )
    for c, value in enumerate((one, two, three)):
        out_ref[:, c, 0, 0] = value.astype(BF16).reshape(32, 16, 128)


def vmem():
    return pl.BlockSpec(memory_space=pltpu.VMEM)


def ring_scratch(width):
    return [
        pltpu.VMEM((8, 2, 96, width), BF16),
        pltpu.VMEM((2, 4, 2, 96, width), BF16),
        pltpu.VMEM((96, width), BF16),
    ]


def run_main(w, y, res, shift, scale, qkv, grad, sout):
    dma = pltpu.SemaphoreType.DMA
    return pl.pallas_call(
        main_kernel,
        out_shape=(
            jax.ShapeDtypeStruct((8, 128, 256), BF16),
            jax.ShapeDtypeStruct((128, 3072), BF16),
            jax.ShapeDtypeStruct((96, 768), F32),
            jax.ShapeDtypeStruct((8, 4, 96, 256), BF16),
        ),
        in_specs=[vmem()] * 8,
        out_specs=(vmem(),) * 4,
        scratch_shapes=[
            pltpu.VMEM((32, 96, 1024), BF16),
            pltpu.VMEM((8, 128, 3072), BF16),
            pltpu.VMEM((1024, 768), BF16),
            pltpu.VMEM((1024, 128), F32),
            pltpu.VMEM((1024, 128), F32),
            pltpu.VMEM((8, 128, 3072), BF16),
            pltpu.VMEM((4, 64, 3072), BF16),
            pltpu.VMEM((3, 2, 32, 3072), BF16),
            pltpu.VMEM((3, 2, 64, 3072), BF16),
            pltpu.VMEM((64, 3072), BF16),
            pltpu.VMEM((8, 4, 96, 768), BF16),
            *ring_scratch(768),
            pltpu.VMEM((8, 128, 3072), BF16),
            dma((110,)),
            dma((110,)),
            dma((8, 2)),
            dma((8, 2)),
        ],
        compiler_params=pltpu.CompilerParams(
            collective_id=0, has_side_effects=True, vmem_limit_bytes=63 << 20
        ),
        name="main",
    )(w, y, res, shift, scale, qkv, grad, sout)


def run_ws(part):
    dma = pltpu.SemaphoreType.DMA
    return pl.pallas_call(
        ws_kernel,
        out_shape=jax.ShapeDtypeStruct((96, 256), F32),
        in_specs=[vmem()],
        out_specs=vmem(),
        scratch_shapes=[
            pltpu.VMEM((8, 4, 96, 256), BF16),
            *ring_scratch(256),
            dma((20,)),
            dma((20,)),
            dma((8, 2)),
            dma((8, 2)),
        ],
        compiler_params=pltpu.CompilerParams(
            collective_id=1, has_side_effects=True, vmem_limit_bytes=16 << 20
        ),
        name="ws_sum",
    )(part)


def run_spatial(qkv, grad):
    return pl.pallas_call(
        spatial_kernel,
        grid=(2, 2),
        out_shape=jax.ShapeDtypeStruct((32, 3, 2, 2, 16, 128), BF16),
        in_specs=[
            pl.BlockSpec((3, 1, 1, 512, 128), lambda h, f: (0, h, f, 0, 0)),
            pl.BlockSpec((1, 512, 128), lambda h, f: (f, 0, h)),
        ],
        out_specs=pl.BlockSpec((32, 3, 1, 1, 16, 128), lambda h, f: (0, 0, h, f, 0, 0)),
        compiler_params=pltpu.CompilerParams(vmem_limit_bytes=32 << 20),
        name="spatial",
    )(qkv, grad)


def local(
    y_rows, grad_res, shift, scale_mod, temporal_qkv, temporal_grad,
    spatial_qkv, spatial_out, w_temporal, w_spatial,
):
    w = jnp.concatenate(
        [
            jnp.transpose(w_temporal, (1, 0, 2, 3)).reshape(96, 768),
            jnp.transpose(w_spatial, (1, 0, 2)).reshape(96, 256),
        ],
        axis=1,
    )
    gso, ig, wt, ws_part = run_main(
        w,
        y_rows.reshape(128, 3072),
        grad_res.reshape(128, 3072),
        shift.reshape(1, 3072),
        scale_mod.reshape(1, 3072),
        temporal_qkv.reshape(3, 2, 1024, 128),
        temporal_grad.reshape(2, 1024, 128),
        spatial_out.reshape(2, 1024, 128),
    )
    by_frames = lax.all_to_all(
        gso.reshape(64, 16, 256), "pos", split_axis=0, concat_axis=1, tiled=True
    )
    grads = run_spatial(spatial_qkv, by_frames)
    moved = lax.all_to_all(grads, "pos", split_axis=0, concat_axis=0, tiled=True)
    ws = run_ws(ws_part)
    by_heads = jnp.transpose(moved, (1, 2, 0, 3, 4, 5)).reshape(3, 2, 64, 16, 128)
    wt = jnp.transpose(wt.reshape(96, 2, 3, 128), (1, 0, 2, 3))
    ws = jnp.transpose(ws.reshape(96, 2, 128), (1, 0, 2))
    return by_heads, ig.reshape(8, 16, 3072), wt, ws


def solution(mesh):
    placed = (
        P("seq", "pos", None),
        P("seq", "pos", None),
        P(),
        P(),
        P(None, "seq", None, "pos", None),
        P("seq", None, "pos", None),
        P(None, "seq", "pos", None, None),
        P("seq", None, "pos", None),
        P("seq", "pos", None, None),
        P("seq", "pos", None),
    )
    return jax.shard_map(
        local,
        mesh=mesh,
        in_specs=placed,
        out_specs=(
            P(None, "seq", None, "pos", None),
            P("seq", "pos", None),
            P("seq", "pos", None, None),
            P("seq", "pos", None),
        ),
        check_vma=False,
    )
```

time: 888 us -> 272 us (0.31)
  waiting for transfers between devices: 703 us -> 0.01 us
  Pallas kernels: 0 us -> 222 us
  matrix products: 80.5 us -> 0 us
  blocking collectives: 0 us -> 31.7 us
  other arithmetic: 31.1 us -> 0.7 us
  local copies, waits for them, and re-layouts: 26.8 us -> 7.38 us
  starting transfers between devices: 21.1 us -> 5.86 us
  between operations: 15.3 us -> 0.73 us
    all_gather x4 -> x0, waiting for transfers between devices: 290 us -> none  [the longest x1 81.4 us: local(): lax.all_gather(w_temporal, 'pos', axis=1, tiled=True)]
    unnamed x8 -> x0, waiting for transfers between devices: 243 us -> none
    pallas_call x0 -> x3, Pallas kernels: none -> 222 us  [the longest x1 162 us: run_main(): pl.pallas_call(main_kernel, out_shape=(jax.ShapeDtypeStruct((8, 128, 256)...]
    reduce_scatter x2 -> x0, waiting for transfers between devices: 171 us -> none  [the longest x1 114 us: local(): lax.psum_scatter(spatial_wgrad.astype(jnp.bfloat16), 'pos', scatter_dimen...]
    dot_general x13 -> x0, matrix products: 79 us -> none  [the longest x1 20.8 us: local(): jnp.einsum('fpd,chfpe->hdce', normed, grads_t, preferred_element_type=jnp...]
    all_to_all x0 -> x1, blocking collectives: none -> 31.7 us  [local(): lax.all_to_all(gso.reshape(64, 16, 256), 'pos', split_axis=0, concat_axis...]
    convert_element_type x4 -> x0, other arithmetic: 18.9 us -> none  [the longest x1 13.4 us: normalize(): normed = (unit_rows * (1.0 + scale_mod) + shift).astype(jnp.bfloat16)]
    all_to_all x2 -> x1, starting transfers between devices: 19.8 us -> 5.86 us  [local(): lax.all_to_all(grads, 'pos', split_axis=0, concat_axis=0, tiled=True)]
  transfers between devices with their start and end apart: 9 -> 1, of which waited for: 7 -> 0; matrix products, arithmetic and copies ran while one was open for 14% -> 1% of each run, Pallas kernels for 0% -> 20%
where the time goes in v1:
time: 272 us; the launch traced here: 268 us
  Pallas kernels  222 us (82%)
  blocking collectives  31.7 us (12%)
  local copies, waits for them, and re-layouts  7.38 us (3%)
  starting transfers between devices  5.86 us (2%)
    pallas_call x1, Pallas kernels, run_main(): pl.pallas_call(main_kernel, out_shape=(jax.ShapeDtypeStruct((8, 128, 256)...  162 us
    pallas_call x1, Pallas kernels, run_ws(): pl.pallas_call(ws_kernel, out_shape=jax.ShapeDtypeStruct((96, 256), F32),...  52.9 us
    all_to_all x1, blocking collectives, local(): lax.all_to_all(gso.reshape(64, 16, 256), 'pos', split_axis=0, concat_axis...  31.7 us
    pallas_call x1, Pallas kernels, run_spatial(): pl.pallas_call(spatial_kernel, grid=(2, 2), out_shape=jax.ShapeDtypeStruc...  6.65 us
    all_to_all x1, starting transfers between devices, local(): lax.all_to_all(grads, 'pos', split_axis=0, concat_axis=0, tiled=True)  5.86 us
  transfers between devices with their start and end apart: 1, of which 0 were waited for; matrix products, arithmetic and copies ran while one was open for 1% of the time, Pallas kernels for 20%

profile of v1, /device:TPU:1, one launch (start us, length us, event | category | flops | bytes accessed | tf_op | source)
XLA Modules:
  0.0 268.3 jit_solution(16032467810001809981)
XLA Ops:
  0.6 0.0 copy-start
  0.6 0.8 copy-done
  1.4 1.0 copy.18
  2.5 0.1 reshape.50
  2.6 0.7 pad_maximum_fusion.w_ref
  3.3 162.4 %main.1 = (bf16[8,128,256]{2,1,0:T(8,128)(2,1)}, bf16[128,3072]{1,0:T(8,128)(2,1)}, f32[96,768]{1,0:T(8,128)}, bf16[8,4,96,256]{3,2,1,0:T(8,128)(2,1)}) custom-call(bf16[96,1024]{1,0:T(8,128)(2,1)} %pad_maximum_fusion.w_ref, bf16[128,3072]{1,0:T(8,128)(2,1)} %bitcast.36, bf16[128,3072]{1,0:T(8,128)(2,1)} %bitcast.37, f32[1,3072]{1,0:T(1,128)} %bitcast.42, ...), custom_call_target="tpu_custom_call" | custom-call | tf_op jit(solution)/shard_map/main/pallas_call | solution.py:591
  165.7 0.0 copy-start.1
  165.7 31.7 %all_to_all.23 = bf16[64,16,256]{2,1,0:T(8,128)(2,1)S(1)} all-to-all(bf16[64,16,256]{2,1,0:T(8,128)(2,1)} %bitcast.40), channel_id=1, replica_groups=mesh['seq'=8,'pos'=32] {'pos'}, dimensions={0} | all-to-all | bytes 1048576 | tf_op jit(solution)/shard_map/all_to_all | solution.py:685
  197.4 0.0 copy-done.1
  197.4 6.6 %spatial.1 = bf16[32,3,2,2,16,128]{5,4,3,2,1,0:T(8,128)(2,1)} custom-call(bf16[3,2,2,512,128]{4,3,2,1,0:T(8,128)(2,1)S(1)} %copy-done.1, bf16[2,512,256]{2,1,0:T(8,128)(2,1)S(1)} %bitcast.30), custom_call_target="tpu_custom_call" | custom-call | tf_op jit(solution)/shard_map/spatial/pallas_call | solution.py:650
  204.1 0.0 copy-start.2
  204.1 5.9 %all-to-all-start.1 = ((bf16[32,3,2,2,16,128]{5,4,3,2,1,0:T(8,128)(2,1)}), bf16[32,3,2,2,16,128]{5,4,3,2,1,0:T(8,128)(2,1)}, u32[]{:S(2)}, u32[]{:S(2)}) async-start(bf16[32,3,2,2,16,128]{5,4,3,2,1,0:T(8,128)(2,1)} %spatial.1), calls=%async_computation.1 | async-start | bytes 3145728 | tf_op jit(solution)/shard_map/all_to_all | solution.py:689
  210.0 0.0 copy-start.4
  210.0 0.0 copy-done.2
  210.0 52.9 %ws_sum.1 = f32[96,256]{1,0:T(8,128)S(1)} custom-call(bf16[8,4,96,256]{3,2,1,0:T(8,128)(2,1)S(1)} %copy-done.2), custom_call_target="tpu_custom_call" | custom-call | tf_op jit(solution)/shard_map/ws_sum/pallas_call | solution.py:629
  262.8 0.0 copy-done.4
  262.8 0.2 reshape.62
  263.0 0.8 copy.23
  263.8 0.6 bitcast_bitcast_fusion
  264.4 0.0 all-to-all-done.1
  264.4 0.0 copy-start.3
  264.4 2.9 %copy.21 = bf16[3,2,32,2,16,128]{5,4,3,2,1,0:T(8,128)(2,1)} copy(bf16[3,2,32,2,16,128]{5,4,3,1,0,2:T(8,128)(2,1)} %bitcast.13) | data formatting | bytes 3145728 | tf_op jit(solution)/shard_map/transpose | solution.py:691
  267.4 0.0 copy-done.3
  267.4 0.9 copy.29
  (2 shorter events, 0.0 us)
Async XLA Ops:
  0.6 0.8 copy-start
  165.7 31.7 %copy-start.1 = (bf16[3,2,2,512,128]{4,3,2,1,0:T(8,128)(2,1)S(1)}, bf16[3,2,2,512,128]{4,3,2,1,0:T(8,128)(2,1)}, u32[]{:S(2)}) copy-start(bf16[3,2,2,512,128]{4,3,2,1,0:T(8,128)(2,1)} %qkv_ref.1) | copy-start | bytes 4718596
  204.1 5.9 %copy-start.2 = (bf16[8,4,96,256]{3,2,1,0:T(8,128)(2,1)S(1)}, bf16[8,4,96,256]{3,2,1,0:T(8,128)(2,1)}, u32[]{:S(2)}) copy-start(bf16[8,4,96,256]{3,2,1,0:T(8,128)(2,1)} %get-tuple-element.11.part_in) | copy-start | bytes 4718596
  204.1 60.4 %all-to-all-start.1 = ((bf16[32,3,2,2,16,128]{5,4,3,2,1,0:T(8,128)(2,1)}), bf16[32,3,2,2,16,128]{5,4,3,2,1,0:T(8,128)(2,1)}, u32[]{:S(2)}, u32[]{:S(2)}) async-start(bf16[32,3,2,2,16,128]{5,4,3,2,1,0:T(8,128)(2,1)} %spatial.1), calls=%async_computation.1 | async-start | bytes 3145728 | tf_op jit(solution)/shard_map/all_to_all | solution.py:689
  210.0 52.9 %copy-start.4 = (f32[96,768]{1,0:T(8,128)S(1)}, f32[96,768]{1,0:T(8,128)}, u32[]{:S(2)}) copy-start(f32[96,768]{1,0:T(8,128)} %get-tuple-element.10) | copy-start | bytes 884740
  264.4 2.9 %copy-start.3 = (bf16[128,3072]{1,0:T(8,128)(2,1)S(1)}, bf16[128,3072]{1,0:T(8,128)(2,1)}, u32[]{:S(2)}) copy-start(bf16[128,3072]{1,0:T(8,128)(2,1)} %get-tuple-element.9) | copy-start | bytes 2359300

commit v2 on v1

--- a/solution.py
+++ b/solution.py
@@ -58,6 +58,20 @@
     for device in devices:
         pl.semaphore_signal(barrier, inc=1, device_id=device, device_id_type=MESH)
     pl.semaphore_wait(barrier, len(devices))
+
+
+def meet_all(me):
+    barrier = pltpu.get_barrier_semaphore()
+    for device in me.neighbours(True, False):
+        pl.semaphore_signal(barrier, inc=1, device_id=device, device_id_type=MESH)
+    s, p = lax.axis_index("seq"), lax.axis_index("pos")
+
+    def body(i, carry):
+        pl.semaphore_signal(barrier, inc=1, device_id=(s, (p + i) % 32), device_id_type=MESH)
+        return carry
+
+    lax.fori_loop(1, 32, body, 0)
+    pl.semaphore_wait(barrier, 34)
 
 
 class Net:
@@ -372,17 +386,20 @@
 
 
 def main_kernel(
-    w_ref, y_ref, res_ref, shift_ref, scale_ref, qkv_ref, grad_ref, sout_ref,
-    gso_ref, ig_ref, wt_ref, ws_ref,
+    w_ref, y_ref, res_ref, shift_ref, scale_ref, qkv_ref, grad_ref, sout_ref, sqkv_ref,
+    out_ref, ig_ref, wt_ref, ws_ref,
     wf, nf, dq, dk, dv, part, from_y, quarter, half, last_y,
     wpart, core_recv, ring, across, igf,
-    send_sem, recv_sem, core_send, core_recv_sem,
+    gso, byf, gout, wspart, core_recv_s, ring_s, across_s,
+    send_sem, recv_sem, core_send, core_recv_sem, core_send_s, core_recv_sem_s,
+    gso_send, gso_recv, out_send, out_recv,
 ):
     me = Place()
     net = Net(send_sem, recv_sem)
     s_own = me.yl * 4 + me.x
+    p_own = lax.axis_index("pos")
     far = 1 - me.yl
-    meet(me.neighbours(True, True))
+    meet_all(me)
 
     first = gather_pos(net, me, w_ref, wf)
     next(first)
@@ -501,7 +518,15 @@
     lax.fori_loop(0, 4, functools.partial(back_tile, lower=True), 0)
     lax.fori_loop(0, 4, functools.partial(back_tile, lower=False), 0)
 
-    pending = []
+    def gso_copy(p_to, p_from):
+        return pltpu.make_async_remote_copy(
+            src_ref=gso.at[p_to],
+            dst_ref=byf.at[p_from],
+            send_sem=gso_send.at[p_to],
+            recv_sem=gso_recv.at[p_from],
+            device_id=(s_own, p_to),
+            device_id_type=MESH,
+        )
 
     def project(blocks):
         def body(i, carry):
@@ -509,11 +534,24 @@
             for n in range(1, len(blocks)):
                 s = jnp.where(i == n, blocks[n], s)
             w = wf[:, :, pl.ds(768, 256)].reshape(3072, 256)
-            gso_ref[s] = dot(igf[s], w).astype(BF16)
+            result = dot(igf[s], w).astype(BF16).reshape(4, 32, 256)
+            gso[pl.ds(s * 4, 4)] = result
+            for n in range(4):
+                p_to = s * 4 + n
+
+                @pl.when(p_to == p_own)
+                def _():
+                    byf[p_to] = result[n]
+
+                @pl.when(p_to != p_own)
+                def _():
+                    gso_copy(p_to, p_own).start()
+
             return carry
 
         lax.fori_loop(0, len(blocks), body, 0)
 
+    pending = []
     last = gather_seq(net, me, igf, lambda at: pending.append(at[0] * 4 + at[1]))
     live = [last, wt_steps]
     while live:
@@ -522,56 +560,80 @@
                 next(step)
             except StopIteration:
                 live.remove(step)
-            if len(pending) >= 3 or (step is last and last not in live):
+            if pending:
                 project(pending)
                 pending.clear()
 
-    def ws_tile(z, carry):
-        at = pl.ds(pl.multiple_of(z * 384, 128), 384)
-        left = igf[:, :, at].reshape(1024, 384)
-        for h in range(2):
-            ws_ref[z, :, :, pl.ds(h * 128, 128)] = (
-                dot(left, sout_ref[h], TN).astype(BF16).reshape(4, 96, 128)
-            )
-        return carry
-
-    lax.fori_loop(0, 8, ws_tile, 0)
-    for pair in core:
+    weight_partial(
+        me, igf, lambda: sout_ref[...], wspart, core_recv_s, core_send_s, core_recv_sem_s
+    )
+    core_s = core_copies_of(me, wspart, core_recv_s, core_send_s, core_recv_sem_s)
+    ws_steps = reduce_pos_ring(
+        net, me, wspart, core_recv_s, core_s, ring_s, across_s, ws_ref
+    )
+    next(ws_steps)
+
+    def others(body):
+        def step(i, carry):
+            body((p_own + i) % 32)
+            return carry
+
+        lax.fori_loop(1, 32, step, 0)
+
+    others(lambda p: gso_copy(p_own, p).wait_recv())
+
+    def out_copy(h, p_to, p_from):
+        return pltpu.make_async_remote_copy(
+            src_ref=gout.at[p_to, h],
+            dst_ref=out_ref.at[:, h, p_from],
+            send_sem=out_send.at[h, p_to],
+            recv_sem=out_recv.at[h, p_from],
+            device_id=(s_own, p_to),
+            device_id_type=MESH,
+        )
+
+    for h in range(2):
+        spatial(h, sqkv_ref, byf, dk, dv, gout)
+        out_ref[:, h, p_own] = gout[p_own, h]
+        others(lambda p: out_copy(h, p, p_own).start())
+        next(ws_steps)
+    for _ in ws_steps:
+        pass
+    for h in range(2):
+        others(lambda p: out_copy(h, p_own, p).wait_recv())
+    for h in range(2):
+        others(lambda p: out_copy(h, p, p_own).wait_send())
+    others(lambda p: gso_copy(p, p_own).wait_send())
+    for pair in core + core_s:
         for copy in pair.copies:
             copy.wait_send()
     net.finish()
 
 
-def ws_kernel(
-    part_in, out_ref, part, core_recv, ring, across, send_sem, recv_sem, core_send, core_recv_sem
-):
-    me = Place()
-    net = Net(send_sem, recv_sem)
-    meet(me.neighbours(False, True))
-
-    def body(i, carry):
-        zt = (me.z + z_order(i)) % 8
-        part[zt] = part_in[zt]
-        for copy in core_copy(me, part, core_recv, core_send, core_recv_sem, zt, i):
-            copy.start()
+def spatial(h, qkv, byf, dk, dv, gout):
+    tile = 256
+
+    def frame(f, carry):
+        def rows(t, inner):
+            at = pl.ds(pl.multiple_of(t * tile, tile), tile)
+            blocks = pl.ds(t * (tile // 16), tile // 16)
+            g = byf[blocks, pl.ds(f * 16, 16), pl.ds(h * 128, 128)].reshape(tile, 128)
+            one, two, three = attention_rows(
+                qkv[0, h, f, at, :], qkv[1, h, f], qkv[2, h, f], g, None
+            )
+            gout[blocks, h, 0, f] = one.astype(BF16).reshape(tile // 16, 16, 128)
+            dk[:512] += two
+            dv[:512] += three
+            return inner
+
+        dk[:512] = jnp.zeros((512, 128), F32)
+        dv[:512] = jnp.zeros((512, 128), F32)
+        lax.fori_loop(0, 512 // tile, rows, 0)
+        gout[:, h, 1, f] = dk[:512].astype(BF16).reshape(32, 16, 128)
+        gout[:, h, 2, f] = dv[:512].astype(BF16).reshape(32, 16, 128)
         return carry
 
-    lax.fori_loop(0, 8, body, 0)
-    core = core_copies_of(me, part, core_recv, core_send, core_recv_sem)
-    for _ in reduce_pos_ring(net, me, part, core_recv, core, ring, across, out_ref):
-        pass
-    for pair in core:
-        for copy in pair.copies:
-            copy.wait_send()
-    net.finish()
-
-
-def spatial_kernel(qkv_ref, grad_ref, out_ref):
-    one, two, three = attention_rows(
-        qkv_ref[0, 0, 0], qkv_ref[1, 0, 0], qkv_ref[2, 0, 0], grad_ref[0], None
-    )
-    for c, value in enumerate((one, two, three)):
-        out_ref[:, c, 0, 0] = value.astype(BF16).reshape(32, 16, 128)
+    lax.fori_loop(0, 2, frame, 0)
 
 
 def vmem():
@@ -586,17 +648,17 @@
     ]
 
 
-def run_main(w, y, res, shift, scale, qkv, grad, sout):
+def run_main(w, y, res, shift, scale, qkv, grad, sout, sqkv):
     dma = pltpu.SemaphoreType.DMA
     return pl.pallas_call(
         main_kernel,
         out_shape=(
-            jax.ShapeDtypeStruct((8, 128, 256), BF16),
+            jax.ShapeDtypeStruct((3, 2, 32, 2, 16, 128), BF16),
             jax.ShapeDtypeStruct((128, 3072), BF16),
             jax.ShapeDtypeStruct((96, 768), F32),
-            jax.ShapeDtypeStruct((8, 4, 96, 256), BF16),
+            jax.ShapeDtypeStruct((96, 256), F32),
         ),
-        in_specs=[vmem()] * 8,
+        in_specs=[vmem()] * 9,
         out_specs=(vmem(),) * 4,
         scratch_shapes=[
             pltpu.VMEM((32, 96, 1024), BF16),
@@ -612,53 +674,27 @@
             pltpu.VMEM((8, 4, 96, 768), BF16),
             *ring_scratch(768),
             pltpu.VMEM((8, 128, 3072), BF16),
-            dma((110,)),
-            dma((110,)),
+            pltpu.VMEM((32, 32, 256), BF16),
+            pltpu.VMEM((32, 32, 256), BF16),
+            pltpu.VMEM((32, 2, 3, 2, 16, 128), BF16),
+            pltpu.VMEM((8, 4, 96, 256), BF16),
+            *ring_scratch(256),
+            dma((130,)),
+            dma((130,)),
             dma((8, 2)),
             dma((8, 2)),
+            dma((8, 2)),
+            dma((8, 2)),
+            dma((32,)),
+            dma((32,)),
+            dma((2, 32)),
+            dma((2, 32)),
         ],
         compiler_params=pltpu.CompilerParams(
             collective_id=0, has_side_effects=True, vmem_limit_bytes=63 << 20
         ),
         name="main",
-    )(w, y, res, shift, scale, qkv, grad, sout)
-
-
-def run_ws(part):
-    dma = pltpu.SemaphoreType.DMA
-    return pl.pallas_call(
-        ws_kernel,
-        out_shape=jax.ShapeDtypeStruct((96, 256), F32),
-        in_specs=[vmem()],
-        out_specs=vmem(),
-        scratch_shapes=[
-            pltpu.VMEM((8, 4, 96, 256), BF16),
-            *ring_scratch(256),
-            dma((20,)),
-            dma((20,)),
-            dma((8, 2)),
-            dma((8, 2)),
-        ],
-        compiler_params=pltpu.CompilerParams(
-            collective_id=1, has_side_effects=True, vmem_limit_bytes=16 << 20
-        ),
-        name="ws_sum",
-    )(part)
-
-
-def run_spatial(qkv, grad):
-    return pl.pallas_call(
-        spatial_kernel,
-        grid=(2, 2),
-        out_shape=jax.ShapeDtypeStruct((32, 3, 2, 2, 16, 128), BF16),
-        in_specs=[
-            pl.BlockSpec((3, 1, 1, 512, 128), lambda h, f: (0, h, f, 0, 0)),
-            pl.BlockSpec((1, 512, 128), lambda h, f: (f, 0, h)),
-        ],
-        out_specs=pl.BlockSpec((32, 3, 1, 1, 16, 128), lambda h, f: (0, 0, h, f, 0, 0)),
-        compiler_params=pltpu.CompilerParams(vmem_limit_bytes=32 << 20),
-        name="spatial",
-    )(qkv, grad)
+    )(w, y, res, shift, scale, qkv, grad, sout, sqkv)
 
 
 def local(
@@ -672,7 +708,7 @@
         ],
         axis=1,
     )
-    gso, ig, wt, ws_part = run_main(
+    grads, ig, wt, ws = run_main(
         w,
         y_rows.reshape(128, 3072),
         grad_res.reshape(128, 3072),
@@ -680,15 +716,10 @@
         scale_mod.reshape(1, 3072),
         temporal_qkv.reshape(3, 2, 1024, 128),
         temporal_grad.reshape(2, 1024, 128),
-        spatial_out.reshape(2, 1024, 128),
+        jnp.transpose(spatial_out, (1, 2, 0, 3)).reshape(1024, 256),
+        spatial_qkv,
     )
-    by_frames = lax.all_to_all(
-        gso.reshape(64, 16, 256), "pos", split_axis=0, concat_axis=1, tiled=True
-    )
-    grads = run_spatial(spatial_qkv, by_frames)
-    moved = lax.all_to_all(grads, "pos", split_axis=0, concat_axis=0, tiled=True)
-    ws = run_ws(ws_part)
-    by_heads = jnp.transpose(moved, (1, 2, 0, 3, 4, 5)).reshape(3, 2, 64, 16, 128)
+    by_heads = grads.reshape(3, 2, 64, 16, 128)
     wt = jnp.transpose(wt.reshape(96, 2, 3, 128), (1, 0, 2, 3))
     ws = jnp.transpose(ws.reshape(96, 2, 128), (1, 0, 2))
     return by_heads, ig.reshape(8, 16, 3072), wt, ws

time: 272 us -> 250 us (0.919)
  blocking collectives: 31.7 us -> 0 us
  Pallas kernels: 222 us -> 237 us
  starting transfers between devices: 5.86 us -> 0 us
  local copies, waits for them, and re-layouts: 7.38 us -> 10.5 us
    all_to_all x1 -> x0, blocking collectives: 31.7 us -> none  [local(): lax.all_to_all(gso.reshape(64, 16, 256), 'pos', split_axis=0, concat_axis...]
    pallas_call x3 -> x1, Pallas kernels: 222 us -> 237 us  [run_main(): pl.pallas_call(main_kernel, out_shape=(jax.ShapeDtypeStruct((3, 2, 32, 2,...]
    all_to_all x1 -> x0, starting transfers between devices: 5.86 us -> none  [local(): lax.all_to_all(grads, 'pos', split_axis=0, concat_axis=0, tiled=True)]
  transfers between devices with their start and end apart: 1 -> 0, of which waited for: 0 -> 0; matrix products, arithmetic and copies ran while one was open for 1% -> 0% of each run, Pallas kernels for 20% -> 0%
where the time goes in v2:
time: 250 us; the launch traced here: 248 us
  Pallas kernels  237 us (95%)
  local copies, waits for them, and re-layouts  10.5 us (4%)
    pallas_call x1, Pallas kernels, run_main(): pl.pallas_call(main_kernel, out_shape=(jax.ShapeDtypeStruct((3, 2, 32, 2,...  237 us
    unnamed x10, local copies, waits for them, and re-layouts  5 us

profile of v2, /device:TPU:1, one launch (start us, length us, event | category | flops | bytes accessed | tf_op | source)
XLA Modules:
  0.0 248.4 jit_solution(5087383377367197470)
XLA Ops:
  0.6 0.0 copy-start
  0.6 0.8 copy-done
  1.4 1.0 copy.19
  2.5 0.1 reshape.47
  2.6 0.7 pad_maximum_fusion.w_ref
  3.3 1.6 copy.21
  4.9 0.9 copy.30
  5.7 236.5 %main.1 = (bf16[3,2,32,2,16,128]{5,4,3,2,1,0:T(8,128)(2,1)}, bf16[128,3072]{1,0:T(8,128)(2,1)}, f32[96,768]{1,0:T(8,128)}, f32[96,256]{1,0:T(8,128)}) custom-call(bf16[96,1024]{1,0:T(8,128)(2,1)} %pad_maximum_fusion.w_ref, bf16[128,3072]{1,0:T(8,128)(2,1)} %bitcast.35, bf16[128,3072]{1,0:T(8,128)(2,1)} %bitcast.36, f32[1,3072]{1,0:T(1,128)} %bitcast.40, ...), custom_call_target="tpu_custom_call" | custom-call | tf_op jit(solution)/shard_map/main/pallas_call | solution.py:653
  242.3 0.0 copy-start.1
  242.3 1.7 bitcast_bitcast_fusion
  244.0 1.1 reshape.58
  245.1 0.8 copy.23
  245.8 0.0 copy-done.1
  245.8 0.0 copy-start.2
  245.8 1.1 copy.33
  247.0 0.5 copy-done.2
  247.5 0.9 copy.34
  (1 shorter events, 0.0 us)
Async XLA Ops:
  0.6 0.8 copy-start
  242.3 3.6 %copy-start.1 = (bf16[3,2,32,2,16,128]{5,4,3,2,1,0:T(8,128)(2,1)S(1)}, bf16[3,2,32,2,16,128]{5,4,3,2,1,0:T(8,128)(2,1)}, u32[]{:S(2)}) copy-start(bf16[3,2,32,2,16,128]{5,4,3,2,1,0:T(8,128)(2,1)} %get-tuple-element.8) | copy-start | bytes 4718596
  245.8 1.7 copy-start.2

commit v3 on v2

--- a/solution.py
+++ b/solution.py
@@ -58,20 +58,6 @@
     for device in devices:
         pl.semaphore_signal(barrier, inc=1, device_id=device, device_id_type=MESH)
     pl.semaphore_wait(barrier, len(devices))
-
-
-def meet_all(me):
-    barrier = pltpu.get_barrier_semaphore()
-    for device in me.neighbours(True, False):
-        pl.semaphore_signal(barrier, inc=1, device_id=device, device_id_type=MESH)
-    s, p = lax.axis_index("seq"), lax.axis_index("pos")
-
-    def body(i, carry):
-        pl.semaphore_signal(barrier, inc=1, device_id=(s, (p + i) % 32), device_id_type=MESH)
-        return carry
-
-    lax.fori_loop(1, 32, body, 0)
-    pl.semaphore_wait(barrier, 34)
 
 
 class Net:
@@ -99,16 +85,6 @@
         self.open = []
 
 
-def run_all(steps):
-    live = list(steps)
-    while live:
-        for step in list(live):
-            try:
-                next(step)
-            except StopIteration:
-                live.remove(step)
-
-
 def add_into(target, terms, rows, tile=16):
     def body(i, carry):
         at = pl.ds(pl.multiple_of(i * tile, tile), tile)
@@ -121,18 +97,17 @@
     lax.fori_loop(0, rows // tile, body, 0)
 
 
-def gather_pos(net, me, own, full):
+def gather_pos(net, me, full):
     def slot(z, r, co):
         return full.at[z * 4 + ((me.yh + r) % 2) * 2 + co]
 
     up, down = me.at(z=me.dz(1)), me.at(z=me.dz(-1))
     other = me.at(co=1 - me.co)
     mine = slot(me.z, 0, me.co)
-    cross = net.send(own, mine, me.at(yh=1 - me.yh))
-    plus = [net.send(own, mine, up)]
-    minus = [net.send(own, mine, down)]
-    cores = [net.send(own, mine, other)]
-    mine[...] = own[...]
+    cross = net.send(mine, mine, me.at(yh=1 - me.yh))
+    plus = [net.send(mine, mine, up)]
+    minus = [net.send(mine, mine, down)]
+    cores = [net.send(mine, mine, other)]
     yield
     cross.wait_recv()
     near = slot(me.z, 1, me.co)
@@ -159,8 +134,10 @@
                 else:
                     next_minus.append(None)
                 cores.append(net.send(block, block, other))
+            if k < 4:
+                yield
         plus, minus = next_plus, next_minus
-        yield
+    yield
     for copy in cores:
         copy.wait_recv()
 
@@ -289,7 +266,44 @@
             swap = net.send(slot(me.z, 1), across, me.at(yh=1 - me.yh))
     yield
     swap.wait_recv()
-    out[...] = slot(me.z, 0)[...].astype(F32) + across[...].astype(F32)
+    out(slot(me.z, 0)[...].astype(F32) + across[...].astype(F32))
+
+
+def reduce_pos_direct(net, me, part, core_recv, core_copies, from_yh, from_z, out):
+    def slot(z, r):
+        return part.at[z, ((me.yh + r) % 2) * 2 + me.co]
+
+    for i in range(8):
+        core_copies[i].wait_recv()
+
+    def merge(z, carry):
+        for r in range(2):
+            add_into(slot(z, r), [core_recv.at[z, (me.yh + r) % 2]], 96)
+        return carry
+
+    lax.fori_loop(0, 8, merge, 0)
+    swap = net.send(
+        part.at[:, (1 - me.yh) * 2 + me.co], from_yh, me.at(yh=1 - me.yh)
+    )
+    yield
+    swap.wait_recv()
+
+    def join(z, carry):
+        add_into(slot(z, 0), [from_yh.at[z]], 96)
+        return carry
+
+    lax.fori_loop(0, 8, join, 0)
+    copies = [
+        net.send(slot(me.dz(k), 0), from_z.at[me.z], me.at(z=me.dz(k)))
+        for k in (4, 3, 5, 2, 6, 1, 7)
+    ]
+    yield
+    for copy in copies:
+        copy.wait_recv()
+    total = slot(me.z, 0)[...].astype(F32)
+    for k in range(1, 8):
+        total += from_z[me.dz(k)].astype(F32)
+    out(total)
 
 
 def z_order(i):
@@ -386,23 +400,29 @@
 
 
 def main_kernel(
-    w_ref, y_ref, res_ref, shift_ref, scale_ref, qkv_ref, grad_ref, sout_ref, sqkv_ref,
+    w_ref, v_ref, y_ref, res_ref, shift_ref, scale_ref, qkv_ref, grad_ref, sout_ref, sqkv_ref,
     out_ref, ig_ref, wt_ref, ws_ref,
     wf, nf, dq, dk, dv, part, from_y, quarter, half, last_y,
     wpart, core_recv, ring, across, igf,
-    gso, byf, gout, wspart, core_recv_s, ring_s, across_s,
+    gso, byf, gout, wspart, core_recv_s, from_yh, from_z,
     send_sem, recv_sem, core_send, core_recv_sem, core_send_s, core_recv_sem_s,
     gso_send, gso_recv, out_send, out_recv,
+    qkv, grad, res, sout, sqkv, local_sem,
 ):
     me = Place()
     net = Net(send_sem, recv_sem)
     s_own = me.yl * 4 + me.x
     p_own = lax.axis_index("pos")
     far = 1 - me.yl
-    meet_all(me)
-
-    first = gather_pos(net, me, w_ref, wf)
-    next(first)
+    local_copies = [
+        pltpu.make_async_copy(source, target, local_sem.at[i])
+        for i, (source, target) in enumerate(
+            [(qkv_ref, qkv), (grad_ref, grad), (res_ref, res), (sout_ref, sout), (sqkv_ref, sqkv)]
+        )
+    ]
+    for copy in local_copies:
+        copy.start()
+    meet(me.neighbours(True, True))
 
     def norm_tile(i, carry):
         at = pl.ds(pl.multiple_of(i * 16, 16), 16)
@@ -410,16 +430,32 @@
         nf[s_own, at, :] = (unit * (1.0 + scale_ref[...]) + shift_ref[...]).astype(BF16)
         return carry
 
+    for h in range(2):
+        for c in range(3):
+            wf[p_own, :, pl.ds((h * 3 + c) * 128, 128)] = w_ref[h, c]
+        wf[p_own, :, pl.ds(768 + h * 128, 128)] = v_ref[h]
+    first = gather_pos(net, me, wf)
+    second = gather_seq(net, me, nf, lambda at: None)
+    next(first)
     lax.fori_loop(0, 8, norm_tile, 0)
-    second = gather_seq(net, me, nf, lambda at: None)
+    next(second)
+    for copy in local_copies[:2]:
+        copy.wait()
+    temporal(0, qkv, grad, dk, dv, dq)
+    next(first)
+    next(first)
+    temporal(1, qkv, grad, dk, dv, dq)
+    next(first)
+    next(first)
+    next(second)
     next(second)
     next(first)
-
-    temporal(0, qkv_ref, grad_ref, dk, dv, dq)
+    next(first)
+    next(first)
     next(second)
-    next(first)
-    temporal(1, qkv_ref, grad_ref, dk, dv, dq)
-    run_all([first, second])
+    next(second)
+    for _ in first:
+        pass
 
     def partial(x):
         lhs = jnp.concatenate(
@@ -470,9 +506,21 @@
     next(red_far)
     next(red_own)
 
+    for _ in second:
+        pass
     weight_partial(me, nf, lambda: dq[...], wpart, core_recv, core_send, core_recv_sem)
     core = core_copies_of(me, wpart, core_recv, core_send, core_recv_sem)
-    wt_steps = reduce_pos_ring(net, me, wpart, core_recv, core, ring, across, wt_ref)
+
+    def wt_total(value):
+        for h in range(2):
+            for c in range(3):
+                wt_ref[h, c] = value[:, (h * 3 + c) * 128 : (h * 3 + c + 1) * 128]
+
+    def ws_total(value):
+        for h in range(2):
+            ws_ref[h] = value[:, h * 128 : (h + 1) * 128]
+
+    wt_steps = reduce_pos_ring(net, me, wpart, core_recv, core, ring, across, wt_total)
 
     for i in range(4):
         swaps[i].wait_recv()
@@ -494,6 +542,9 @@
         pass
     swap.wait_recv()
 
+    for copy in local_copies[2:]:
+        copy.wait()
+
     def back_tile(i, carry, lower):
         base = 0 if lower else 64
         at = pl.ds(pl.multiple_of(i * 16 + base, 16), 16)
@@ -509,7 +560,7 @@
         scaled = total * (1.0 + scale_ref[...])
         one = jnp.mean(scaled, axis=-1, keepdims=True)
         two = jnp.mean(scaled * unit, axis=-1, keepdims=True)
-        result = res_ref[at, :].astype(F32) + inverse * (scaled - one - unit * two)
+        result = res[at, :].astype(F32) + inverse * (scaled - one - unit * two)
         result = result.astype(BF16)
         igf[s_own, at, :] = result
         ig_ref[at, :] = result
@@ -551,36 +602,12 @@
 
         lax.fori_loop(0, len(blocks), body, 0)
 
-    pending = []
-    last = gather_seq(net, me, igf, lambda at: pending.append(at[0] * 4 + at[1]))
-    live = [last, wt_steps]
-    while live:
-        for step in list(live):
-            try:
-                next(step)
-            except StopIteration:
-                live.remove(step)
-            if pending:
-                project(pending)
-                pending.clear()
-
-    weight_partial(
-        me, igf, lambda: sout_ref[...], wspart, core_recv_s, core_send_s, core_recv_sem_s
-    )
-    core_s = core_copies_of(me, wspart, core_recv_s, core_send_s, core_recv_sem_s)
-    ws_steps = reduce_pos_ring(
-        net, me, wspart, core_recv_s, core_s, ring_s, across_s, ws_ref
-    )
-    next(ws_steps)
-
     def others(body):
         def step(i, carry):
             body((p_own + i) % 32)
             return carry
 
         lax.fori_loop(1, 32, step, 0)
-
-    others(lambda p: gso_copy(p_own, p).wait_recv())
 
     def out_copy(h, p_to, p_from):
         return pltpu.make_async_remote_copy(
@@ -592,11 +619,57 @@
             device_id_type=MESH,
         )
 
-    for h in range(2):
-        spatial(h, sqkv_ref, byf, dk, dv, gout)
+    def attend(h):
+        if h == 0:
+            others(lambda p: gso_copy(p_own, p).wait_recv())
+        spatial(h, sqkv, byf, dk, dv, gout)
         out_ref[:, h, p_own] = gout[p_own, h]
         others(lambda p: out_copy(h, p, p_own).start())
-        next(ws_steps)
+
+    pending = []
+
+    def come():
+        blocks = list(pending)
+        pending.clear()
+        project(blocks)
+        return blocks
+
+    last = gather_seq(net, me, igf, lambda at: pending.append(at[0] * 4 + at[1]))
+    next(last)
+    come()
+    next(wt_steps)
+    next(last)
+    next(last)
+    come()
+    next(wt_steps)
+    next(last)
+    next(last)
+    come()
+    for _ in wt_steps:
+        pass
+    next(last)
+    come()
+    for _ in last:
+        pass
+    come()
+
+    weight_partial(
+        me,
+        igf,
+        lambda: jnp.concatenate([sout[0], sout[1]], axis=1),
+        wspart,
+        core_recv_s,
+        core_send_s,
+        core_recv_sem_s,
+    )
+    core_s = core_copies_of(me, wspart, core_recv_s, core_send_s, core_recv_sem_s)
+    ws_steps = reduce_pos_direct(
+        net, me, wspart, core_recv_s, core_s, from_yh, from_z, ws_total
+    )
+    next(ws_steps)
+    for h in range(2):
+        attend(h)
+        next(ws_steps, None)
     for _ in ws_steps:
         pass
     for h in range(2):
@@ -640,6 +713,10 @@
     return pl.BlockSpec(memory_space=pltpu.VMEM)
 
 
+def anywhere():
+    return pl.BlockSpec(memory_space=pl.ANY)
+
+
 def ring_scratch(width):
     return [
         pltpu.VMEM((8, 2, 96, width), BF16),
@@ -648,17 +725,17 @@
     ]
 
 
-def run_main(w, y, res, shift, scale, qkv, grad, sout, sqkv):
+def run_main(w, v, y, res, shift, scale, qkv, grad, sout, sqkv):
     dma = pltpu.SemaphoreType.DMA
     return pl.pallas_call(
         main_kernel,
         out_shape=(
             jax.ShapeDtypeStruct((3, 2, 32, 2, 16, 128), BF16),
             jax.ShapeDtypeStruct((128, 3072), BF16),
-            jax.ShapeDtypeStruct((96, 768), F32),
-            jax.ShapeDtypeStruct((96, 256), F32),
+            jax.ShapeDtypeStruct((2, 3, 96, 128), F32),
+            jax.ShapeDtypeStruct((2, 96, 128), F32),
         ),
-        in_specs=[vmem()] * 9,
+        in_specs=[vmem(), vmem(), vmem(), anywhere(), vmem(), vmem()] + [anywhere()] * 4,
         out_specs=(vmem(),) * 4,
         scratch_shapes=[
             pltpu.VMEM((32, 96, 1024), BF16),
@@ -678,7 +755,9 @@
             pltpu.VMEM((32, 32, 256), BF16),
             pltpu.VMEM((32, 2, 3, 2, 16, 128), BF16),
             pltpu.VMEM((8, 4, 96, 256), BF16),
-            *ring_scratch(256),
+            pltpu.VMEM((8, 2, 96, 256), BF16),
+            pltpu.VMEM((8, 96, 256), BF16),
+            pltpu.VMEM((8, 96, 256), BF16),
             dma((130,)),
             dma((130,)),
             dma((8, 2)),
@@ -689,39 +768,38 @@
             dma((32,)),
             dma((2, 32)),
             dma((2, 32)),
+            pltpu.VMEM((3, 2, 1024, 128), BF16),
+            pltpu.VMEM((2, 1024, 128), BF16),
+            pltpu.VMEM((128, 3072), BF16),
+            pltpu.VMEM((2, 1024, 128), BF16),
+            pltpu.VMEM((3, 2, 2, 512, 128), BF16),
+            dma((5,)),
         ],
         compiler_params=pltpu.CompilerParams(
             collective_id=0, has_side_effects=True, vmem_limit_bytes=63 << 20
         ),
         name="main",
-    )(w, y, res, shift, scale, qkv, grad, sout, sqkv)
+    )(w, v, y, res, shift, scale, qkv, grad, sout, sqkv)
 
 
 def local(
     y_rows, grad_res, shift, scale_mod, temporal_qkv, temporal_grad,
     spatial_qkv, spatial_out, w_temporal, w_spatial,
 ):
-    w = jnp.concatenate(
-        [
-            jnp.transpose(w_temporal, (1, 0, 2, 3)).reshape(96, 768),
-            jnp.transpose(w_spatial, (1, 0, 2)).reshape(96, 256),
-        ],
-        axis=1,
-    )
     grads, ig, wt, ws = run_main(
-        w,
+        jnp.transpose(w_temporal, (0, 2, 1, 3)),
+        w_spatial,
         y_rows.reshape(128, 3072),
         grad_res.reshape(128, 3072),
         shift.reshape(1, 3072),
         scale_mod.reshape(1, 3072),
         temporal_qkv.reshape(3, 2, 1024, 128),
         temporal_grad.reshape(2, 1024, 128),
-        jnp.transpose(spatial_out, (1, 2, 0, 3)).reshape(1024, 256),
+        spatial_out.reshape(2, 1024, 128),
         spatial_qkv,
     )
     by_heads = grads.reshape(3, 2, 64, 16, 128)
-    wt = jnp.transpose(wt.reshape(96, 2, 3, 128), (1, 0, 2, 3))
-    ws = jnp.transpose(ws.reshape(96, 2, 128), (1, 0, 2))
+    wt = jnp.transpose(wt, (0, 2, 1, 3))
     return by_heads, ig.reshape(8, 16, 3072), wt, ws
 
 

time: 250 us -> 233 us (0.932)
  Pallas kernels: 237 us -> 227 us
  local copies, waits for them, and re-layouts: 10.5 us -> 5.38 us
    pallas_call x1, Pallas kernels: 237 us -> 227 us  [run_main(): pl.pallas_call(main_kernel, out_shape=(jax.ShapeDtypeStruct((3, 2, 32, 2,...]
    transpose x3 -> x0, local copies, waits for them, and re-layouts: 4.25 us -> none  [the longest x1 1.66 us: local(): ws = jnp.transpose(ws.reshape(96, 2, 128), (1, 0, 2))]
where the time goes in v3:
time: 233 us
  Pallas kernels  227 us (97%)
  local copies, waits for them, and re-layouts  5.38 us (2%)
    pallas_call x1, Pallas kernels, run_main(): pl.pallas_call(main_kernel, out_shape=(jax.ShapeDtypeStruct((3, 2, 32, 2,...  227 us
    unnamed x10, local copies, waits for them, and re-layouts  5.38 us

profile of v3, /device:TPU:1, one launch (start us, length us, event | category | flops | bytes accessed | tf_op | source)
XLA Modules:
  0.0 232.7 jit_solution(11447518163718754288)
XLA Ops:
  0.6 226.6 %main.1 = (bf16[3,2,32,2,16,128]{5,4,3,2,1,0:T(8,128)(2,1)}, bf16[128,3072]{1,0:T(8,128)(2,1)}, f32[2,3,96,128]{3,2,1,0:T(8,128)}, f32[2,96,128]{2,1,0:T(8,128)}) custom-call(bf16[2,3,96,128]{3,2,1,0:T(8,128)(2,1)} %bitcast.19, bf16[2,96,128]{2,1,0:T(8,128)(2,1)} %v_ref.1, bf16[128,3072]{1,0:T(8,128)(2,1)} %bitcast.14, bf16[128,3072]{1,0:T(8,128)(2,1)} %bitcast.15, ...), custom_call_target="tpu_custom_call" | custom-call | tf_op jit(solution)/shard_map/main/pallas_call | solution.py:730
  227.3 0.0 copy-start
  227.3 2.9 %copy.18 = bf16[3,2,64,16,128]{4,3,2,1,0:T(8,128)(2,1)} copy(bf16[3,2,64,16,128]{4,3,2,1,0:T(8,128)(2,1)} %bitcast.11) | data formatting | bytes 3145728
  230.2 0.0 copy-done
  230.2 0.0 copy-start.1
  230.2 0.0 copy-start.2
  230.2 0.9 copy.19
  231.1 0.2 copy-done.1
  231.3 0.7 copy.20
  232.0 0.0 copy-done.2
  232.0 0.6 copy.21
Async XLA Ops:
  227.3 2.9 %copy-start = (bf16[128,3072]{1,0:T(8,128)(2,1)S(1)}, bf16[128,3072]{1,0:T(8,128)(2,1)}, u32[]{:S(2)}) copy-start(bf16[128,3072]{1,0:T(8,128)(2,1)} %get-tuple-element.9) | copy-start | bytes 2359300
  230.2 1.1 copy-start.1
  230.2 1.8 copy-start.2

commit v4 on v3

--- a/solution.py
+++ b/solution.py
@@ -1,5 +1,3 @@
-import functools
-
 import jax
 import jax.numpy as jnp
 from jax import lax
@@ -13,6 +11,7 @@
 NT = (((1,), (1,)), ((), ()))
 TN = (((0,), (0,)), ((), ()))
 NN = (((1,), (0,)), ((), ()))
+CUT, REST = 14 * 128, 10 * 128
 
 
 def dot(a, b, dims=NN):
@@ -143,8 +142,8 @@
 
 
 def gather_seq(net, me, full, done):
-    def part(yl, x, first, rows):
-        return full.at[yl * 4 + x, pl.ds(first, rows), :]
+    def part(yl, x, first, width):
+        return full.at[yl * 4 + x, :, pl.ds(first, width)]
 
     yl, x, far = me.yl, me.x, 1 - me.yl
     left, right, xo = me.dx(-1), me.dx(1), me.dx(2)
@@ -153,72 +152,79 @@
     def push(block, device):
         return net.send(block, block, device)
 
-    h0, h1 = part(yl, x, 0, 64), part(yl, x, 64, 64)
-    y0 = push(h0, to_y)
-    r0, l0 = push(h0, to_r), push(h0, to_l)
-    y1 = push(h1, to_y)
-    r1, l1 = push(h1, to_r), push(h1, to_l)
+    def low(yl, x):
+        return part(yl, x, 0, CUT)
+
+    def high(yl, x):
+        return part(yl, x, CUT, REST)
+
+    y0, y1 = push(low(yl, x), to_y), push(high(yl, x), to_y)
+    r1, l1 = push(high(yl, x), to_r), push(high(yl, x), to_l)
+    r0, l0 = push(low(yl, x), to_r), push(low(yl, x), to_l)
     done((yl, x))
     yield
+    r1.wait_recv()
+    rc = push(part(yl, left, CUT, REST // 2), to_r)
+    yr = push(high(yl, left), to_y)
+    l1.wait_recv()
+    ld = push(part(yl, right, CUT + REST // 2, REST // 2), to_l)
+    yq = push(high(yl, right), to_y)
+    yield
     y0.wait_recv()
-    f0 = part(far, x, 0, 64)
-    rf, lf = push(f0, to_r), push(f0, to_l)
+    rf, lf = push(low(far, x), to_r), push(low(far, x), to_l)
+    yield
     r0.wait_recv()
+    ra = push(part(yl, left, 0, CUT // 2), to_r)
     l0.wait_recv()
-    ra = push(part(yl, left, 0, 32), to_r)
-    lb = push(part(yl, right, 32, 32), to_l)
+    lb = push(part(yl, right, CUT // 2, CUT // 2), to_l)
     y1.wait_recv()
     done((far, x))
-    yield
-    r1.wait_recv()
-    l1.wait_recv()
-    rc = push(part(yl, left, 64, 32), to_r)
-    ld = push(part(yl, right, 96, 32), to_l)
-    yr = push(part(yl, left, 64, 64), to_y)
-    yq = push(part(yl, right, 64, 64), to_y)
     done((yl, left))
     done((yl, right))
     yield
-    rf.wait_recv()
-    lf.wait_recv()
-    re = push(part(far, left, 0, 32), to_r)
-    lg = push(part(far, right, 32, 32), to_l)
-    ra.wait_recv()
-    lb.wait_recv()
-    yield
     rc.wait_recv()
     ld.wait_recv()
-    yo = push(part(yl, xo, 64, 64), to_y)
-    done((yl, xo))
-    yield
+    yo = push(high(yl, xo), to_y)
+    yield
+    rf.wait_recv()
+    re = push(part(far, left, 0, CUT // 2), to_r)
+    lf.wait_recv()
+    lg = push(part(far, right, CUT // 2, CUT // 2), to_l)
     yr.wait_recv()
     yq.wait_recv()
     done((far, left))
     done((far, right))
     yield
+    ra.wait_recv()
+    lb.wait_recv()
+    done((yl, xo))
+    yield
     re.wait_recv()
     lg.wait_recv()
     yo.wait_recv()
     done((far, xo))
 
 
-def reduce_x(net, me, block, quarter, half, started, result):
+def reduce_x(net, me, block, width, quarter, half):
     left, right, xo = me.dx(-1), me.dx(1), me.dx(2)
     to_r, to_l = me.at(x=right), me.at(x=left)
-    a = net.send(block(xo).at[pl.ds(0, 32)], quarter.at[0], to_r)
-    b = net.send(block(xo).at[pl.ds(32, 32)], quarter.at[1], to_l)
-    started()
+    one, two = pl.ds(0, width // 2), pl.ds(width // 2, width // 2)
+    whole = pl.ds(0, width)
+    near = [quarter.at[n, :, one] for n in range(2)]
+    sums = [half.at[n, :, whole] for n in range(2)]
+    a = net.send(block(xo).at[:, one], near[0], to_r)
+    b = net.send(block(xo).at[:, two], near[1], to_l)
     yield
     a.wait_recv()
-    add_into(block(right).at[pl.ds(0, 32)], [quarter.at[0]], 32)
-    c = net.send(block(right), half.at[0], to_r)
+    add_into(block(right).at[:, one], [near[0]], 128)
+    c = net.send(block(right), sums[0], to_r)
     b.wait_recv()
-    add_into(block(left).at[pl.ds(32, 32)], [quarter.at[1]], 32)
-    d = net.send(block(left), half.at[1], to_l)
+    add_into(block(left).at[:, two], [near[1]], 128)
+    d = net.send(block(left), sums[1], to_l)
     yield
     c.wait_recv()
     d.wait_recv()
-    result()
+    add_into(block(me.x), sums, 128)
 
 
 def reduce_pos_ring(net, me, part, core_recv, core_copies, ring, across, out):
@@ -444,15 +450,16 @@
     temporal(0, qkv, grad, dk, dv, dq)
     next(first)
     next(first)
+    next(second)
+    next(second)
     temporal(1, qkv, grad, dk, dv, dq)
     next(first)
     next(first)
     next(second)
+    next(first)
     next(second)
     next(first)
     next(first)
-    next(first)
-    next(second)
     next(second)
     for _ in first:
         pass
@@ -472,38 +479,34 @@
 
         lax.fori_loop(0, 8, body, 0)
 
-    def h0(yl):
-        return lambda x: part.at[yl * 4 + x, pl.ds(0, 64), :]
-
-    def h1(x):
-        return part.at[me.yl * 4 + x, pl.ds(64, 64), :]
+    def low(yl):
+        return lambda x: part.at[yl * 4 + x, :, pl.ds(0, CUT)]
+
+    def high(x):
+        return part.at[me.yl * 4 + x, :, pl.ds(CUT, REST)]
 
     def to_partner(x):
-        return net.send(
-            part.at[far * 4 + x, pl.ds(64, 64), :], from_y.at[x], me.at(yl=far)
-        )
-
-    nothing = lambda: None
+        return net.send(part.at[far * 4 + x, :, pl.ds(CUT, REST)], from_y.at[x], me.at(yl=far))
+
+    def take(i):
+        swaps[i].wait_recv()
+        add_into(high(order[i]), [from_y.at[order[i]]], 128)
+
     swaps = {}
     order = [me.dx(2), me.dx(1), me.dx(-1), me.x]
+    red_far = reduce_x(net, me, low(far), CUT, quarter.at[0], half.at[0])
+    red_own = reduce_x(net, me, low(me.yl), CUT, quarter.at[1], half.at[1])
+    red_two = reduce_x(net, me, high, REST, quarter.at[2], half.at[2])
     partial(order[0])
-    keep = {}
-
-    def ready(name):
-        def mark():
-            keep[name] = True
-
-        return mark
-
-    red_far = reduce_x(net, me, h0(far), quarter.at[0], half.at[0], nothing, ready("far"))
     next(red_far)
     swaps[0] = to_partner(order[0])
-    red_own = reduce_x(net, me, h0(me.yl), quarter.at[1], half.at[1], nothing, ready("own"))
     next(red_own)
     for i in range(1, 4):
         partial(order[i])
         swaps[i] = to_partner(order[i])
     next(red_far)
+    take(0)
+    next(red_two)
     next(red_own)
 
     for _ in second:
@@ -522,20 +525,15 @@
 
     wt_steps = reduce_pos_ring(net, me, wpart, core_recv, core, ring, across, wt_total)
 
-    for i in range(4):
-        swaps[i].wait_recv()
-        add_into(h1(order[i]), [from_y.at[order[i]]], 64)
-        if i == 0:
-            red_two = reduce_x(net, me, h1, quarter.at[2], half.at[2], nothing, ready("two"))
-            next(red_two)
-            next(wt_steps)
-    next(red_two)
+    take(1)
+    take(2)
+    next(wt_steps)
     for _ in red_far:
         pass
-    mine = part.at[far * 4 + me.x, pl.ds(0, 64), :]
-    add_into(mine, [half.at[0, 0], half.at[0, 1]], 64)
-    swap = net.send(mine, last_y, me.at(yl=far))
+    swap = net.send(part.at[far * 4 + me.x, :, pl.ds(0, CUT)], last_y, me.at(yl=far))
+    next(red_two)
     next(wt_steps)
+    take(3)
     for _ in red_own:
         pass
     for _ in red_two:
@@ -545,17 +543,11 @@
     for copy in local_copies[2:]:
         copy.wait()
 
-    def back_tile(i, carry, lower):
-        base = 0 if lower else 64
-        at = pl.ds(pl.multiple_of(i * 16 + base, 16), 16)
-        sub = pl.ds(pl.multiple_of(i * 16, 16), 16)
+    def back_tile(i, carry):
+        at = pl.ds(pl.multiple_of(i * 16, 16), 16)
         total = part[s_own, at, :].astype(F32)
-        if lower:
-            terms = [half.at[1, 0], half.at[1, 1], last_y]
-        else:
-            terms = [half.at[2, 0], half.at[2, 1]]
-        for term in terms:
-            total += term[sub, :].astype(F32)
+        more = total[:, :CUT] + last_y[at, :].astype(F32)
+        total = jnp.concatenate([more, total[:, CUT:]], axis=1)
         unit, inverse = unit_of(y_ref[at, :])
         scaled = total * (1.0 + scale_ref[...])
         one = jnp.mean(scaled, axis=-1, keepdims=True)
@@ -566,8 +558,7 @@
         ig_ref[at, :] = result
         return carry
 
-    lax.fori_loop(0, 4, functools.partial(back_tile, lower=True), 0)
-    lax.fori_loop(0, 4, functools.partial(back_tile, lower=False), 0)
+    lax.fori_loop(0, 8, back_tile, 0)
 
     def gso_copy(p_to, p_from):
         return pltpu.make_async_remote_copy(
@@ -604,10 +595,10 @@
 
     def others(body):
         def step(i, carry):
-            body((p_own + i) % 32)
+            body((p_own + 16 + (1 - 2 * (i % 2)) * ((i + 1) // 2)) % 32)
             return carry
 
-        lax.fori_loop(1, 32, step, 0)
+        lax.fori_loop(0, 31, step, 0)
 
     def out_copy(h, p_to, p_from):
         return pltpu.make_async_remote_copy(
@@ -640,9 +631,10 @@
     next(wt_steps)
     next(last)
     next(last)
+    next(last)
     come()
+    next(last)
     next(wt_steps)
-    next(last)
     next(last)
     come()
     for _ in wt_steps:
@@ -744,10 +736,10 @@
             pltpu.VMEM((1024, 128), F32),
             pltpu.VMEM((1024, 128), F32),
             pltpu.VMEM((8, 128, 3072), BF16),
-            pltpu.VMEM((4, 64, 3072), BF16),
-            pltpu.VMEM((3, 2, 32, 3072), BF16),
-            pltpu.VMEM((3, 2, 64, 3072), BF16),
-            pltpu.VMEM((64, 3072), BF16),
+            pltpu.VMEM((4, 128, REST), BF16),
+            pltpu.VMEM((3, 2, 128, CUT // 2), BF16),
+            pltpu.VMEM((3, 2, 128, CUT), BF16),
+            pltpu.VMEM((128, CUT), BF16),
             pltpu.VMEM((8, 4, 96, 768), BF16),
             *ring_scratch(768),
             pltpu.VMEM((8, 128, 3072), BF16),

time: 233 us -> 224 us (0.961)
  Pallas kernels: 227 us -> 217 us
    pallas_call x1, Pallas kernels: 227 us -> 217 us  [run_main(): pl.pallas_call(main_kernel, out_shape=(jax.ShapeDtypeStruct((3, 2, 32, 2,...]
where the time goes in v4:
time: 224 us
  Pallas kernels  217 us (97%)
  local copies, waits for them, and re-layouts  5.38 us (2%)
    pallas_call x1, Pallas kernels, run_main(): pl.pallas_call(main_kernel, out_shape=(jax.ShapeDtypeStruct((3, 2, 32, 2,...  217 us
    unnamed x10, local copies, waits for them, and re-layouts  5.38 us

profile of v4, /device:TPU:1, one launch (start us, length us, event | category | flops | bytes accessed | tf_op | source)
XLA Modules:
  0.0 223.5 jit_solution(9909098478554005046)
XLA Ops:
  0.6 217.5 %main.1 = (bf16[3,2,32,2,16,128]{5,4,3,2,1,0:T(8,128)(2,1)}, bf16[128,3072]{1,0:T(8,128)(2,1)}, f32[2,3,96,128]{3,2,1,0:T(8,128)}, f32[2,96,128]{2,1,0:T(8,128)}) custom-call(bf16[2,3,96,128]{3,2,1,0:T(8,128)(2,1)} %bitcast.19, bf16[2,96,128]{2,1,0:T(8,128)(2,1)} %v_ref.1, bf16[128,3072]{1,0:T(8,128)(2,1)} %bitcast.14, bf16[128,3072]{1,0:T(8,128)(2,1)} %bitcast.15, ...), custom_call_target="tpu_custom_call" | custom-call | tf_op jit(solution)/shard_map/main/pallas_call | solution.py:722
  218.1 0.0 copy-start
  218.1 2.9 %copy.18 = bf16[3,2,64,16,128]{4,3,2,1,0:T(8,128)(2,1)} copy(bf16[3,2,64,16,128]{4,3,2,1,0:T(8,128)(2,1)} %bitcast.11) | data formatting | bytes 3145728
  221.0 0.0 copy-done
  221.0 0.0 copy-start.1
  221.0 0.0 copy-start.2
  221.0 0.9 copy.19
  221.9 0.2 copy-done.1
  222.2 0.7 copy.20
  222.9 0.0 copy-done.2
  222.9 0.6 copy.21
Async XLA Ops:
  218.1 2.9 %copy-start = (bf16[128,3072]{1,0:T(8,128)(2,1)S(1)}, bf16[128,3072]{1,0:T(8,128)(2,1)}, u32[]{:S(2)}) copy-start(bf16[128,3072]{1,0:T(8,128)(2,1)} %get-tuple-element.9) | copy-start | bytes 2359300
  221.0 1.1 copy-start.1
  221.0 1.8 copy-start.2

commit v5 on v4

--- a/solution.py
+++ b/solution.py
@@ -375,7 +375,7 @@
     return dot(ds, k), dot(ds, q, TN), dot(p.astype(BF16), g, TN)
 
 
-def temporal(h, qkv, grad, dk, dv, out):
+def temporal(h, piece, qkv, grad, dk, dv, out):
     tile = 128
     rows = lax.broadcasted_iota(jnp.int32, (tile, 1024), 0)
     cols = lax.broadcasted_iota(jnp.int32, (tile, 1024), 1)
@@ -391,9 +391,12 @@
         dv[...] += three
         return carry
 
-    dk[...] = jnp.zeros_like(dk)
-    dv[...] = jnp.zeros_like(dv)
-    lax.fori_loop(0, 1024 // tile, body, 0)
+    if piece == 0:
+        dk[...] = jnp.zeros_like(dk)
+        dv[...] = jnp.zeros_like(dv)
+    lax.fori_loop(piece * 4, piece * 4 + 4, body, 0)
+    if piece == 0:
+        return
     out[:, pl.ds(h * 384 + 128, 128)] = dk[...].astype(BF16)
     out[:, pl.ds(h * 384 + 256, 128)] = dv[...].astype(BF16)
 
@@ -447,15 +450,17 @@
     next(second)
     for copy in local_copies[:2]:
         copy.wait()
-    temporal(0, qkv, grad, dk, dv, dq)
+    temporal(0, 0, qkv, grad, dk, dv, dq)
     next(first)
     next(first)
     next(second)
+    temporal(0, 1, qkv, grad, dk, dv, dq)
     next(second)
-    temporal(1, qkv, grad, dk, dv, dq)
     next(first)
+    temporal(1, 0, qkv, grad, dk, dv, dq)
     next(first)
     next(second)
+    temporal(1, 1, qkv, grad, dk, dv, dq)
     next(first)
     next(second)
     next(first)
@@ -637,13 +642,13 @@
     next(wt_steps)
     next(last)
     come()
-    for _ in wt_steps:
-        pass
     next(last)
     come()
     for _ in last:
         pass
     come()
+    for _ in wt_steps:
+        pass
 
     weight_partial(
         me,

time: 224 us -> 221 us (0.987)
  Pallas kernels: 217 us -> 214 us
    pallas_call x1, Pallas kernels: 217 us -> 214 us  [run_main(): pl.pallas_call(main_kernel, out_shape=(jax.ShapeDtypeStruct((3, 2, 32, 2,...]
where the time goes in v5:
time: 221 us; the launch traced here: 220 us
  Pallas kernels  214 us (97%)
  local copies, waits for them, and re-layouts  5.38 us (2%)
    pallas_call x1, Pallas kernels, run_main(): pl.pallas_call(main_kernel, out_shape=(jax.ShapeDtypeStruct((3, 2, 32, 2,...  214 us
    unnamed x10, local copies, waits for them, and re-layouts  5.38 us

profile of v5, /device:TPU:1, one launch (start us, length us, event | category | flops | bytes accessed | tf_op | source)
XLA Modules:
  0.0 220.4 jit_solution(1814121508353262356)
XLA Ops:
  0.6 214.3 %main.1 = (bf16[3,2,32,2,16,128]{5,4,3,2,1,0:T(8,128)(2,1)}, bf16[128,3072]{1,0:T(8,128)(2,1)}, f32[2,3,96,128]{3,2,1,0:T(8,128)}, f32[2,96,128]{2,1,0:T(8,128)}) custom-call(bf16[2,3,96,128]{3,2,1,0:T(8,128)(2,1)} %bitcast.19, bf16[2,96,128]{2,1,0:T(8,128)(2,1)} %v_ref.1, bf16[128,3072]{1,0:T(8,128)(2,1)} %bitcast.14, bf16[128,3072]{1,0:T(8,128)(2,1)} %bitcast.15, ...), custom_call_target="tpu_custom_call" | custom-call | tf_op jit(solution)/shard_map/main/pallas_call | solution.py:727
  215.0 0.0 copy-start
  215.0 2.9 %copy.18 = bf16[3,2,64,16,128]{4,3,2,1,0:T(8,128)(2,1)} copy(bf16[3,2,64,16,128]{4,3,2,1,0:T(8,128)(2,1)} %bitcast.11) | data formatting | bytes 3145728
  217.9 0.0 copy-done
  217.9 0.0 copy-start.1
  217.9 0.0 copy-start.2
  217.9 0.9 copy.19
  218.8 0.2 copy-done.1
  219.0 0.7 copy.20
  219.7 0.0 copy-done.2
  219.7 0.6 copy.21
Async XLA Ops:
  215.0 2.9 %copy-start = (bf16[128,3072]{1,0:T(8,128)(2,1)S(1)}, bf16[128,3072]{1,0:T(8,128)(2,1)}, u32[]{:S(2)}) copy-start(bf16[128,3072]{1,0:T(8,128)(2,1)} %get-tuple-element.9) | copy-start | bytes 2359300
  217.9 1.1 copy-start.1
  217.9 1.8 copy-start.2
